TPU v7x, 256 devices: a whole 4x4x8 slice. The times are simulated.
256 devices in a mesh: north: 16 (over y, x), east: 8 (over z), group: 2 (over core).
Axes of the slice: x: 4, y: 4, z: 8, core: 2. Of those that a mesh axis runs over, the one named last changes fastest.
Arguments:
- alpha_fields: float32 [16, 8, 1024, 1024], P('group', None, 'north', 'east'), may hold values from -6 to 6
- perturbations: bfloat16 [16, 8, 1024, 1024], P('group', None, 'north', 'east'), may hold values from -6 to 6
- north_filter: float32 [5, 8, 1024], P(None, None, 'north'), may hold values from 0 to 1, as said below
- east_filter: float32 [5, 8, 1024], replicated, may hold values from 0 to 1, as said below
- depth_taps: float32 [5], replicated, may hold values from 0.3 to 1
Outputs:
- increment: float32 [8, 1024, 1024], P(None, 'north', 'east')
Inputs may be any that keep to these rules, and one draw needn't show every extreme that they name: `north_filter`: entry 0 of the first dimension is a cell's gain, entries 1 to 4 its weights on the four preceding cells; the four weights of a cell are positive and sum to less than 1. `east_filter`: entry 0 of the first dimension is a cell's gain, entries 1 to 4 its weights on the four preceding cells; the four weights of a cell are positive and sum to less than 1.
All inputs are finite; a program needn't handle non-finite values.
Results may differ from a plain program's by a relative error of at most 0.0003.
Values may be sent and summed in bfloat16 or wider, within the bound.
No kernel may reach another device: no remote copies, remote signals or barrier semaphores. Data moves between devices by JAX's collectives and lax.ppermute only.
A program may use at most 128 MiB of HBM per device.

v0:
```python
import math

import jax
import jax.numpy as jnp
from jax import lax
from jax.experimental import pallas as pl
from jax.experimental.pallas import tpu as pltpu
from jax.sharding import PartitionSpec as P

F32 = jnp.float32
BF16 = jnp.bfloat16
VMEM = pl.BlockSpec(memory_space=pltpu.VMEM)
SMEM = pl.BlockSpec(memory_space=pltpu.SMEM)
HBM = pl.BlockSpec(memory_space=pltpu.HBM)
MIB = 1 << 20


def split(x):
    high = x.astype(BF16)
    return high, (x - high.astype(F32)).astype(BF16)


def split_rounded(x):
    high = x.astype(BF16).astype(F32)
    return high, x - high


def dot(a, b):
    return jnp.dot(a, b, preferred_element_type=F32)


def dot_nt(a, b):
    return lax.dot_general(a, b, (((1,), (1,)), ((), ())), preferred_element_type=F32)


def wide(column, lanes=128):
    return jnp.broadcast_to(column, (column.shape[0], lanes))


def lanes_of(rows=8, lanes=128):
    return lax.broadcasted_iota(jnp.int32, (rows, lanes), 1)


def rows_of(rows=8, lanes=128):
    return lax.broadcasted_iota(jnp.int32, (rows, lanes), 0)


def copies(source, target, sems, count):
    return [pltpu.make_async_copy(source.at[i], target.at[i], sems.at[i]) for i in range(count)]


def unit(mask):
    return jnp.where(mask, 1.0, 0.0).astype(F32)


def north_functionals(levels, members, rows):
    def kernel(
        nf_hbm, alpha_hbm, p_hbm, s_hbm, nf_ref, alpha_ref, f_ref, s_ref, p_ref, nf_sem, s_sem, sems, p_sems
    ):
        table_fetch = pltpu.make_async_copy(nf_hbm, nf_ref, nf_sem)
        table_fetch.start()
        fetches = copies(alpha_hbm, alpha_ref, sems, members)
        stores = copies(p_ref, p_hbm, p_sems, 2 * levels)
        slab_store = pltpu.make_async_copy(s_ref, s_hbm, s_sem)
        table_fetch.wait()
        for fetch in fetches:
            fetch.start()
        lane = lanes_of()
        table = [nf_ref[j] for j in range(5)]
        gain = jnp.concatenate([jnp.zeros((levels, 64), F32), table[0]], axis=1)
        state = [unit(lane == k) for k in range(4)]
        for i in range(rows):
            value = jnp.where(lane == 64 + i, gain, 0.0)
            for j in (4, 3, 2, 1):
                value = value + wide(table[j][:, i : i + 1]) * state[j - 1]
            f_ref[i] = value + unit(lane == 4 + rows - 1 - i) if i >= rows - 4 else value
            state = [value] + state[:3]
        state = [jnp.zeros((levels, 128), F32)] * 4
        for i in reversed(range(rows)):
            value = f_ref[i]
            for j in (4, 3, 2, 1):
                if i + j < rows:
                    value = value + wide(table[j][:, i + j : i + j + 1]) * state[j - 1]
            s_ref[i] = value * wide(table[0][:, i : i + 1])
            state = [value] + state[:3]
        slab_store.start()
        for fetch in fetches:
            fetch.wait()
        for l in range(levels):
            flat = f_ref[:, l, :]
            maps = jnp.dot(
                flat.T[0:8], flat, precision=lax.Precision.HIGHEST, preferred_element_type=F32
            )
            edge = s_ref[:, l, :].T[0:8]
            high, low = split_rounded(jnp.concatenate([edge, edge], axis=1))
            left = jnp.concatenate([high, low], axis=0).astype(BF16)
            for half in range(2):
                right = []
                for m in range(4):
                    a_high, a_low = split(alpha_ref[half * 4 + m, l])
                    right.append(jnp.concatenate([a_high, a_low], axis=0))
                out = dot(left, jnp.concatenate(right, axis=1))
                out = out[0:8] + out[8:16]
                for m in range(4):
                    p_ref[2 * l + half, 8 * m : 8 * m + 8, :] = out[:, 128 * m : 128 * m + 128]
                p_ref[2 * l + half, 32:40, :] = maps
                stores[2 * l + half].start()
        for store in stores + [slab_store]:
            store.wait()

    def call(north_filter, alpha):
        return pl.pallas_call(
            kernel,
            in_specs=[HBM, HBM],
            out_specs=[HBM, HBM],
            out_shape=[
                jax.ShapeDtypeStruct((2 * levels, 40, 128), F32),
                jax.ShapeDtypeStruct((rows, levels, 128), F32),
            ],
            scratch_shapes=[
                pltpu.VMEM(north_filter.shape, F32),
                pltpu.VMEM(alpha.shape, F32),
                pltpu.VMEM((rows, levels, 128), F32),
                pltpu.VMEM((rows, levels, 128), F32),
                pltpu.VMEM((2 * levels, 40, 128), F32),
                pltpu.SemaphoreType.DMA,
                pltpu.SemaphoreType.DMA,
                pltpu.SemaphoreType.DMA((members,)),
                pltpu.SemaphoreType.DMA((2 * levels,)),
            ],
            compiler_params=pltpu.CompilerParams(vmem_limit_bytes=63 * MIB),
            name="north_functionals",
        )(north_filter, alpha)

    return call


def chain_slabs(received):
    slabs = received.shape[0]

    def kernel(r_ref, z_ref, v_ref):
        state = [jnp.zeros((4, 128), F32)] * 4
        for n in range(slabs):
            maps = r_ref[n, 32:40, :]
            column = [wide(maps[:, j : j + 1]) for j in range(4)]
            for m in range(4):
                z_ref[n, 8 * m : 8 * m + 4, :] = state[m]
                value = r_ref[n, 8 * m : 8 * m + 8, :]
                for j in range(4):
                    value = value + column[j] * jnp.broadcast_to(state[m][j : j + 1], (8, 128))
                v_ref[n, 4 * m : 4 * m + 4, :] = value[0:4]
                state[m] = value[4:8]
        pending = [jnp.zeros((4, 128), F32)] * 4
        for n in reversed(range(slabs)):
            maps = r_ref[n, 32:36, :]
            column = [wide(maps[:, 4 + j : 5 + j]) for j in range(4)]
            for m in range(4):
                z_ref[n, 8 * m + 4 : 8 * m + 8, :] = pending[m]
                value = v_ref[n, 4 * m : 4 * m + 4, :]
                for j in range(4):
                    value = value + column[j] * jnp.broadcast_to(pending[m][j : j + 1], (4, 128))
                pending[m] = value

    return pl.pallas_call(
        kernel,
        in_specs=[VMEM],
        out_specs=VMEM,
        out_shape=jax.ShapeDtypeStruct((slabs, 32, 128), F32),
        scratch_shapes=[pltpu.VMEM((slabs, 16, 128), F32)],
        compiler_params=pltpu.CompilerParams(vmem_limit_bytes=8 * MIB),
        name="chain_slabs",
    )(received)


def north_slab(left, alpha_ref, l, members):
    for first in range(0, members, 4):
        right = []
        for m in range(first, first + 4):
            high, low = split(alpha_ref[m, l])
            right.append(jnp.concatenate([high, low, high, low], axis=0))
        yield first, dot(left, jnp.concatenate(right, axis=1))


def slab_left(full):
    twice = jnp.where(lanes_of(full.shape[0]) < 64, pltpu.roll(full, 64, 1), full)
    high, low = split(twice)
    return jnp.concatenate([high, low], axis=1)


def edge_right(z_ref, l, members):
    right = []
    for m in range(members):
        high, low = split_rounded(z_ref[l, 8 * m : 8 * m + 8, :])
        right.append(jnp.concatenate([high, low, high, low], axis=0).astype(BF16))
    return jnp.concatenate(right, axis=1)


def crossing_rows(v_ref, l, fields):
    parts = jnp.concatenate([jnp.concatenate(split(field), axis=1) for field in fields], axis=0)
    out = dot_nt(jnp.concatenate([v_ref[l], v_ref[l]], axis=1), parts)
    return out[0:32] + out[32:64]


def own_crossing(alpha, slab, sends):
    members, levels, rows, width = alpha.shape

    def kernel(alpha_hbm, s_ref, v_ref, c_ref, u_ref, b_ref, alpha_ref, sems):
        fetches = copies(alpha_hbm, alpha_ref, sems, members)
        for fetch in fetches:
            fetch.start()
        for fetch in fetches:
            fetch.wait()
        lane = lanes_of()
        for l in range(levels):
            full = s_ref[:, l, :]
            fields = []
            for _, out in north_slab(slab_left(full), alpha_ref, l, members):
                fields += [out[:, width * m : width * m + width] for m in range(4)]
            out = crossing_rows(v_ref, l, fields)
            for e in range(8):
                c_ref[e, 4 * l : 4 * l + 4, :] = out[4 * e : 4 * e + 4]
            high, low = split_rounded(full[:, 0:8])
            u_ref[l] = jnp.concatenate([high, high, low, low], axis=1).astype(BF16)
            edge = full.T[0:8]
            edge = jnp.concatenate([edge, edge], axis=1)
            edge = jnp.concatenate([jnp.where(lane < 64, edge, 0.0), jnp.where(lane < 64, 0.0, edge)], axis=0)
            b_ref[l] = jnp.concatenate(split(edge), axis=0)

    return pl.pallas_call(
        kernel,
        in_specs=[HBM, VMEM, VMEM],
        out_specs=[VMEM] * 3,
        scratch_shapes=[pltpu.VMEM(alpha.shape, F32), pltpu.SemaphoreType.DMA((members,))],
        out_shape=[
            jax.ShapeDtypeStruct((8, 4 * levels, members * rows), F32),
            jax.ShapeDtypeStruct((levels, rows, 32), BF16),
            jax.ShapeDtypeStruct((levels, 32, 128), BF16),
        ],
        compiler_params=pltpu.CompilerParams(vmem_limit_bytes=16 * MIB),
        cost_estimate=pl.CostEstimate(flops=2_000_000_000, bytes_accessed=4 * MIB, transcendentals=0),
        name="own_crossing",
    )(alpha, slab, sends)


def east_matrices(place, taps, east_filter, scale):
    levels = east_filter.shape[1]
    length = 128
    slabs = east_filter.shape[2] // length

    def kernel(e_ref, taps_ref, ef_ref, e_out, v_out, w_out, wt_ref, rt_ref, f_ref, s_ref):
        me = e_ref[0]
        lane = lanes_of()
        row = rows_of()
        for j in range(1, 5):
            stacked = jnp.concatenate(
                [ef_ref[j, :, length * s : length * (s + 1)] for s in range(slabs)] * 2, axis=0
            )
            wt_ref[j - 1] = stacked.T
        state = [unit(row == k) for k in range(4)]
        gram = [jnp.zeros((8, 128), F32)] * 4
        for i in range(length):
            value = jnp.zeros((8, 128), F32)
            for j in (3, 2, 1, 0):
                value = value + jnp.broadcast_to(wt_ref[j, i : i + 1, :], (8, 128)) * state[j]
            gram = [gram[k] + value * jnp.broadcast_to(value[k : k + 1], (8, 128)) for k in range(4)]
            state = [value] + state[:3]
        step = state
        reflect = [jnp.zeros((8, 128), F32)] * 4
        for _ in range(slabs - 1):
            inner = [
                sum(jnp.broadcast_to(reflect[i][j : j + 1], (8, 128)) * step[j] for j in range(4))
                for i in range(4)
            ]
            outer = [
                gram[a]
                + sum(jnp.broadcast_to(step[i][a : a + 1], (8, 128)) * inner[i] for i in range(4))
                for a in range(4)
            ]
            reflect = [jnp.where(lane < 56, pltpu.roll(outer[a], 120, 1), 0.0) for a in range(4)]
        rt_ref[...] = jnp.concatenate(reflect * 4, axis=0).T
        back = rt_ref[pl.ds(pl.multiple_of(me * 8, 8), 8), :]
        own = [ef_ref[j, :, pl.ds(pl.multiple_of(me * length, length), length)] for j in range(5)]
        core = [jnp.zeros((levels, 128), F32)] * 4
        side = [unit(lane == k) for k in range(4)]
        for i in range(length):
            weight = [wide(own[j][:, i : i + 1]) for j in range(1, 5)]
            c_value = jnp.where(lane == i, own[0], 0.0)
            s_value = jnp.zeros((levels, 128), F32)
            for j in (3, 2, 1, 0):
                c_value = c_value + weight[j] * core[j]
                s_value = s_value + weight[j] * side[j]
            f_ref[i, :, 0:128] = c_value
            f_ref[i, :, 128:256] = s_value
            core = [c_value] + core[:3]
            side = [s_value] + side[:3]
        for k in range(4):
            c_value, s_value = core[k], side[k]
            for j in range(4):
                weight = wide(back[:, 8 * k + j : 8 * k + j + 1])
                c_value = c_value + weight * core[j]
                s_value = s_value + weight * side[j]
            f_ref[length - 1 - k, :, 0:128] = c_value
            f_ref[length - 1 - k, :, 128:256] = s_value + unit(lane == 4 + k)
        core = [jnp.zeros((levels, 128), F32)] * 4
        side = [jnp.zeros((levels, 128), F32)] * 4
        for i in reversed(range(length)):
            c_value = f_ref[i, :, 0:128]
            s_value = f_ref[i, :, 128:256]
            for j in (4, 3, 2, 1):
                if i + j < length:
                    weight = wide(own[j][:, i + j : i + j + 1])
                    c_value = c_value + weight * core[j - 1]
                    s_value = s_value + weight * side[j - 1]
            gain = wide(own[0][:, i : i + 1])
            s_ref[i, :, 0:128] = c_value * gain
            s_ref[i, :, 128:256] = s_value * gain
            core = [c_value] + core[:3]
            side = [s_value] + side[:3]
        across = [
            jnp.concatenate([step[i][j : j + 1] for i in range(4)], axis=0) for j in range(4)
        ]
        entering, pending = [], []
        for l in range(levels):
            e_high, e_low = split(s_ref[:, l, 0:128])
            e_out[l] = jnp.concatenate([e_high, e_low], axis=0)
            edge = s_ref[:, l, 128:256].T[0:8]
            start, end = edge[0:4], edge[4:8]
            entering.append(start)
            pending.append(end)
            upward = [end]
            for e in range(1, slabs):
                at = 8 * (e - 1) + l
                moved = sum(
                    wide(across[j][:, at : at + 1]) * jnp.broadcast_to(upward[-1][j : j + 1], (4, 128))
                    for j in range(4)
                )
                upward.append(jnp.where(e - 1 > me, moved, end))
            downward = [start]
            for e in reversed(range(slabs - 1)):
                at = 8 * (e + 1) + l
                moved = sum(
                    wide(step[j][0:4, at : at + 1])
                    * jnp.broadcast_to(downward[-1][j : j + 1], (4, 128))
                    for j in range(4)
                )
                downward.append(jnp.where(e + 1 < me, moved, start))
            downward.reverse()
            sends = jnp.concatenate(
                [jnp.where(e > me, upward[e], downward[e]) for e in range(slabs)], axis=0
            )
            high, low = split_rounded(sends)
            v_out[l] = jnp.concatenate([high, low], axis=0).astype(BF16)
        columns = jnp.concatenate(entering + pending, axis=0)
        level = lax.rem(rows_of(64), 32) // 4
        for k in range(levels):
            mix = jnp.zeros((64, 128), F32)
            for offset in range(5):
                mix = mix + jnp.where(level - k == offset - 2, taps_ref[offset] * scale, 0.0)
            high, low = split(columns * mix)
            w_out[:, 128 * k : 128 * k + 128] = jnp.concatenate([high, low], axis=0)

    return pl.pallas_call(
        kernel,
        in_specs=[SMEM, SMEM, VMEM],
        out_specs=[VMEM, VMEM, VMEM],
        out_shape=[
            jax.ShapeDtypeStruct((levels, 2 * length, length), BF16),
            jax.ShapeDtypeStruct((levels, 64, length), BF16),
            jax.ShapeDtypeStruct((128, levels * length), BF16),
        ],
        scratch_shapes=[
            pltpu.VMEM((4, 128, 128), F32),
            pltpu.VMEM((128, 128), F32),
            pltpu.VMEM((length, levels, 256), F32),
            pltpu.VMEM((length, levels, 256), F32),
        ],
        compiler_params=pltpu.CompilerParams(vmem_limit_bytes=16 * MIB),
        cost_estimate=pl.CostEstimate(flops=2_000_000_000, bytes_accessed=4 * MIB, transcendentals=0),
        name="east_matrices",
    )(place, taps, east_filter)


def north_finish(own, edges, entered, sends):
    levels = edges.shape[0]
    pairs = entered.shape[1] // 16

    def kernel(c0_ref, b_ref, z_ref, v_ref, c_hbm, c_ref, sems):
        stores = [
            pltpu.make_async_copy(
                c_ref.at[:, pl.ds(8 * j, 8)], c_hbm.at[:, pl.ds(8 * j, 8)], sems.at[j]
            )
            for j in range(levels // 2)
        ]
        empty = jnp.zeros((16, 128), BF16)
        for l in range(levels):
            values = [
                jnp.concatenate(split(z_ref[l, 16 * p : 16 * p + 16, :]), axis=1) for p in range(pairs)
            ]
            out = dot_nt(
                jnp.concatenate([v_ref[l], v_ref[l]], axis=1), jnp.concatenate(values * 2, axis=0)
            )
            high, low = split_rounded(out[0:32] + out[32:64])
            left = jnp.where(lanes_of(32) < 64, high, low).astype(BF16)
            left = jnp.concatenate([left, left], axis=1)
            blocks = [
                jnp.concatenate(
                    [
                        jnp.concatenate([piece if p == q else empty for q in range(pairs)], axis=1)
                        for p in range(pairs)
                    ],
                    axis=0,
                )
                for piece in (b_ref[l, 0:16], b_ref[l, 16:32])
            ]
            out = dot(left, jnp.concatenate([blocks[0], blocks[0], blocks[1], blocks[1]], axis=0))
            for e in range(8):
                at = slice(4 * l, 4 * l + 4)
                c_ref[e, at, :] = c0_ref[e, at, :] + out[4 * e : 4 * e + 4]
            if l % 2:
                stores[l // 2].start()
        for store in stores:
            store.wait()

    return pl.pallas_call(
        kernel,
        in_specs=[VMEM] * 4,
        out_specs=HBM,
        out_shape=jax.ShapeDtypeStruct(own.shape, F32),
        scratch_shapes=[pltpu.VMEM(own.shape, F32), pltpu.SemaphoreType.DMA((levels // 2,))],
        compiler_params=pltpu.CompilerParams(vmem_limit_bytes=16 * MIB),
        name="north_finish",
    )(own, edges, entered, sends)


def own_increment(taps, alpha, slab, columns, entered, east, perturbations, scale):
    members, levels, rows, width = alpha.shape

    def kernel(taps_ref, alpha_hbm, slab_ref, u_ref, z_ref, e_ref, pert_ref, out_ref, keep_ref, alpha_ref, s_ref, sems):
        fetches = copies(alpha_hbm, alpha_ref, sems, members)
        for fetch in fetches:
            fetch.start()
        for fetch in fetches:
            fetch.wait()
        for l in range(levels):
            added = dot(u_ref[l], edge_right(z_ref, l, members))
            for first, out in north_slab(slab_left(slab_ref[:, l, :]), alpha_ref, l, members):
                out = out + added[:, width * first : width * (first + 4)]
                field = jnp.concatenate([out[:, width * m : width * m + width] for m in range(4)], axis=0)
                high, low = split(field)
                e_high = e_ref[l, 0:width]
                s_ref[l, rows * first : rows * (first + 4)] = dot(
                    jnp.concatenate([high, low], axis=1), jnp.concatenate([e_high, e_high], axis=0)
                ) + dot(high, e_ref[l, width : 2 * width])
        tap = [taps_ref[o] * scale for o in range(5)]
        for k in range(levels):
            total = jnp.zeros((rows, width), F32)
            for m in range(members):
                mixed = sum(
                    tap[o] * s_ref[k + o - 2, rows * m : rows * m + rows, :]
                    for o in range(5)
                    if 0 <= k + o - 2 < levels
                )
                total = total + pert_ref[m, k].astype(F32) * mixed
            out_ref[k] = total
        keep_ref[...] = pert_ref[...]

    return pl.pallas_call(
        kernel,
        in_specs=[SMEM, HBM] + [VMEM] * 5,
        out_specs=[VMEM, VMEM],
        out_shape=[
            jax.ShapeDtypeStruct((levels, rows, width), F32),
            jax.ShapeDtypeStruct(perturbations.shape, BF16),
        ],
        scratch_shapes=[
            pltpu.VMEM(alpha.shape, F32),
            pltpu.VMEM((levels, members * rows, width), F32),
            pltpu.SemaphoreType.DMA((members,)),
        ],
        compiler_params=pltpu.CompilerParams(vmem_limit_bytes=24 * MIB),
        cost_estimate=pl.CostEstimate(flops=2_000_000_000, bytes_accessed=4 * MIB, transcendentals=0),
        name="own_increment",
    )(taps, alpha, slab, columns, entered, east, perturbations)


def finish(place, received, columns, perturbations, partial):
    members, levels, rows, width = perturbations.shape
    slabs = received.shape[0]

    def kernel(e_ref, r_ref, w_ref, pert_ref, part_ref, out_ref):
        me = e_ref[0]
        entering = jnp.zeros(r_ref.shape[1:], F32)
        pending = jnp.zeros(r_ref.shape[1:], F32)
        for s in range(slabs):
            block = r_ref[s]
            entering = entering + jnp.where(s < me, block, 0.0)
            pending = pending + jnp.where(s > me, block, 0.0)
        edge = jnp.concatenate([entering, pending] * 2, axis=0).T
        high, low = split_rounded(edge)
        left = jnp.where(lanes_of(members * rows) < 64, high, low).astype(BF16)
        left = jnp.concatenate([left, left], axis=1)
        for k in range(levels):
            out_ref[k] = part_ref[k]
        high, low = w_ref[0:64], w_ref[64:128]
        right = jnp.concatenate([high, high, low, low], axis=0)
        for m in range(members):
            added = dot(left[rows * m : rows * m + rows], right)
            for k in range(levels):
                out_ref[k] += pert_ref[m, k].astype(F32) * added[:, width * k : width * k + width]

    return pl.pallas_call(
        kernel,
        in_specs=[SMEM] + [VMEM] * 4,
        out_specs=VMEM,
        out_shape=jax.ShapeDtypeStruct((levels, rows, width), F32),
        compiler_params=pltpu.CompilerParams(vmem_limit_bytes=16 * MIB),
        name="finish",
    )(place, received, columns, perturbations, partial)


def local(alpha_fields, perturbations, north_filter, east_filter, depth_taps):
    members, levels, rows, width = alpha_fields.shape
    scale = 1.0 / math.sqrt(members * lax.axis_size("group") - 1)
    place = jnp.full((1,), lax.axis_index("east"), jnp.int32)
    functionals, slab = north_functionals(levels, members, rows)(north_filter, alpha_fields)
    gathered = lax.all_to_all(functionals, "north", 0, 0)
    east, sends, columns = east_matrices(place, depth_taps, east_filter, scale)
    gathered, sends = lax.optimization_barrier((gathered, sends))
    chained, slab = lax.optimization_barrier((chain_slabs(gathered), slab))
    entered = lax.all_to_all(chained, "north", 0, 0).reshape(levels, 8 * members, width)
    own, edge, blocks = own_crossing(alpha_fields, slab, sends)
    crossing = north_finish(own, blocks, entered, sends)
    crossing, entered = lax.optimization_barrier((crossing, entered))
    crossed = lax.all_to_all(crossing, "east", 0, 0)
    partial, kept = own_increment(depth_taps, alpha_fields, slab, edge, entered, east, perturbations, scale)
    increment = finish(place, crossed, columns, kept, partial)
    return increment + lax.ppermute(increment, "group", [(0, 1), (1, 0)])


def solution(mesh):
    placed = (
        P("group", None, "north", "east"),
        P("group", None, "north", "east"),
        P(None, None, "north"),
        P(),
        P(),
    )
    return jax.shard_map(
        local, mesh=mesh, in_specs=placed, out_specs=P(None, "north", "east"), check_vma=False
    )
```

profile of v0, /device:TPU:1, one launch (start us, length us, event | category | flops | bytes accessed | tf_op | source)
XLA Modules:
  0.0 65.6 jit_solution(5426904298287240527)
XLA Ops:
  0.0 0.0 copy-start.7
  0.0 0.0 copy-start.6
  0.0 4.0 %north_functionals.1 = (f32[16,40,128]{2,1,0:T(8,128)}, f32[64,8,128]{2,1,0:T(8,128)}) custom-call(f32[5,8,64]{2,1,0:T(8,128)} %nf_hbm.1, f32[8,8,64,128]{3,2,1,0:T(8,128)} %alpha_hbm.5), custom_call_target="tpu_custom_call" | custom-call | tf_op jit(solution)/shard_map/north_functionals/pallas_call | solution.py:112
  4.0 7.6 %all-to-all-start = ((f32[16,40,128]{2,1,0:T(8,128)}), f32[16,40,128]{2,1,0:T(8,128)S(1)}, u32[]{:S(2)}, u32[]{:S(2)}) async-start(f32[16,40,128]{2,1,0:T(8,128)} %get-tuple-element.21), calls=%async_computation | async-start | bytes 655360 | tf_op jit(solution)/shard_map/all_to_all | solution.py:526
  11.6 0.0 copy-done.7
  11.6 0.0 copy-done.6
  11.6 0.0 copy-start
  11.7 5.0 %east_matrices.1 = (bf16[8,256,128]{2,1,0:T(8,128)(2,1)S(1)}, bf16[8,64,128]{2,1,0:T(8,128)(2,1)S(1)}, bf16[128,1024]{1,0:T(8,128)(2,1)S(1)}) custom-call(s32[1]{0:T(128)} %bitcast.e_ref, f32[5]{0:T(128)S(1)} %copy-done.7, f32[5,8,1024]{2,1,0:T(8,128)S(1)} %copy-done.6), custom_call_target="tpu_custom_call" | custom-call | flops 2000000000 | bytes 4194304 | tf_op jit(solution)/shard_map/east_matrices/pallas_call | solution.py:362
  16.7 0.0 copy-start.8
  16.7 0.8 %copy-done.8 = bf16[8,256,128]{2,1,0:T(8,128)(2,1)} copy-done((bf16[8,256,128]{2,1,0:T(8,128)(2,1)}, bf16[8,256,128]{2,1,0:T(8,128)(2,1)S(1)}, u32[]{:S(2)}) %copy-start.8) | copy-done | bytes 524312
  17.5 2.6 %all-to-all-done.r_ref = f32[16,40,128]{2,1,0:T(8,128)S(1)} async-done(((f32[16,40,128]{2,1,0:T(8,128)}), f32[16,40,128]{2,1,0:T(8,128)S(1)}, u32[]{:S(2)}, u32[]{:S(2)}) %all-to-all-start) | async-done | bytes 327712 | tf_op jit(solution)/shard_map/all_to_all | solution.py:526
  20.1 1.0 %chain_slabs.1 = f32[16,32,128]{2,1,0:T(8,128)} custom-call(f32[16,40,128]{2,1,0:T(8,128)S(1)} %all-to-all-done.r_ref), custom_call_target="tpu_custom_call" | custom-call | tf_op jit(solution)/shard_map/chain_slabs/pallas_call | solution.py:164
  21.1 4.0 %all-to-all-start.1 = ((f32[16,32,128]{2,1,0:T(8,128)}), f32[16,32,128]{2,1,0:T(8,128)S(1)}, u32[]{:S(2)}, u32[]{:S(2)}) async-start(f32[16,32,128]{2,1,0:T(8,128)} %chain_slabs.1), calls=%async_computation.1 | async-start | bytes 524288 | tf_op jit(solution)/shard_map/all_to_all | solution.py:530
  25.2 0.0 copy-done
  25.2 0.0 copy-start.4
  25.2 0.9 %copy-done.4 = f32[64,8,128]{2,1,0:T(8,128)S(1)} copy-done((f32[64,8,128]{2,1,0:T(8,128)S(1)}, f32[64,8,128]{2,1,0:T(8,128)}, u32[]{:S(2)}) %copy-start.4) | copy-done | bytes 262168
  26.1 2.5 %own_crossing.1 = (f32[8,32,512]{2,1,0:T(8,128)S(1)}, bf16[8,64,32]{2,1,0:T(8,128)(2,1)S(1)}, bf16[8,32,128]{2,1,0:T(8,128)(2,1)S(1)}) custom-call(f32[8,8,64,128]{3,2,1,0:T(8,128)S(1)} %copy-done, f32[64,8,128]{2,1,0:T(8,128)S(1)} %copy-done.4, bf16[8,64,128]{2,1,0:T(8,128)(2,1)S(1)} %get-tuple-element.26.v_ref), custom_call_target="tpu_custom_call" | custom-call | flops 2000000000 | bytes 4194304 | tf_op jit(solution)/shard_map/own_crossing/pallas_call | solution.py:229
  28.6 4.1 %all-to-all-done.1 = f32[16,32,128]{2,1,0:T(8,128)S(1)} async-done(((f32[16,32,128]{2,1,0:T(8,128)}), f32[16,32,128]{2,1,0:T(8,128)S(1)}, u32[]{:S(2)}, u32[]{:S(2)}) %all-to-all-start.1) | async-done | bytes 262176 | tf_op jit(solution)/shard_map/all_to_all | solution.py:530
  32.7 2.1 %north_finish.1 = f32[8,32,512]{2,1,0:T(8,128)} custom-call(f32[8,32,512]{2,1,0:T(8,128)S(1)} %get-tuple-element.27.c0_ref, bf16[8,32,128]{2,1,0:T(8,128)(2,1)S(1)} %get-tuple-element.28.b_ref, f32[8,64,128]{2,1,0:T(8,128)S(1)} %bitcast.2, bf16[8,64,128]{2,1,0:T(8,128)(2,1)S(1)} %get-tuple-element.26.v_ref), custom_call_target="tpu_custom_call" | custom-call | tf_op jit(solution)/shard_map/north_finish/pallas_call | solution.py:424
  34.8 8.2 %all-to-all-start.2 = ((f32[8,32,512]{2,1,0:T(8,128)}), f32[8,32,512]{2,1,0:T(8,128)S(1)}, u32[]{:S(2)}, u32[]{:S(2)}) async-start(f32[8,32,512]{2,1,0:T(8,128)} %north_finish.1), calls=%async_computation.2 | async-start | bytes 1048576 | tf_op jit(solution)/shard_map/all_to_all | solution.py:534
  43.0 1.2 %copy-done.3 = bf16[8,8,64,128]{3,2,1,0:T(8,128)(2,1)S(1)} copy-done((bf16[8,8,64,128]{3,2,1,0:T(8,128)(2,1)S(1)}, bf16[8,8,64,128]{3,2,1,0:T(8,128)(2,1)}, u32[]{:S(2)}) %copy-start.3) | copy-done | bytes 1048600
  44.2 0.9 %copy-done.5 = f32[64,8,128]{2,1,0:T(8,128)S(1)} copy-done((f32[64,8,128]{2,1,0:T(8,128)S(1)}, f32[64,8,128]{2,1,0:T(8,128)}, u32[]{:S(2)}) %copy-start.5) | copy-done | bytes 262168
  45.2 1.0 %copy-done.9 = bf16[8,256,128]{2,1,0:T(8,128)(2,1)S(1)} copy-done((bf16[8,256,128]{2,1,0:T(8,128)(2,1)S(1)}, bf16[8,256,128]{2,1,0:T(8,128)(2,1)}, u32[]{:S(2)}) %copy-start.9) | copy-done | bytes 524312
  46.2 3.3 %own_increment.1 = (f32[8,64,128]{2,1,0:T(8,128)S(1)}, bf16[8,8,64,128]{3,2,1,0:T(8,128)(2,1)S(1)}) custom-call(f32[5]{0:T(128)S(1)} %copy-done.7, f32[8,8,64,128]{3,2,1,0:T(8,128)S(1)} %copy-done, f32[64,8,128]{2,1,0:T(8,128)S(1)} %copy-done.5, bf16[8,64,32]{2,1,0:T(8,128)(2,1)S(1)} %get-tuple-element.32.u_ref, f32[8,64,128]{2,1,0:T(8,128)S(1)} %bitcast.3, ...), custom_call_target="tpu_custom_call" | custom-call | flops 2000000000 | bytes 4194304 | tf_op jit(solution)/shard_map/own_increment/pallas_call | solution.py:467
  49.5 0.0 copy-start.1
  49.5 1.0 %copy-done.1 = bf16[8,8,64,128]{3,2,1,0:T(8,128)(2,1)} copy-done((bf16[8,8,64,128]{3,2,1,0:T(8,128)(2,1)}, bf16[8,8,64,128]{3,2,1,0:T(8,128)(2,1)S(1)}, u32[]{:S(2)}) %copy-start.1) | copy-done | bytes 1048600
  50.5 6.9 %all-to-all-done.2.r_ref = f32[8,32,512]{2,1,0:T(8,128)S(1)} async-done(((f32[8,32,512]{2,1,0:T(8,128)}), f32[8,32,512]{2,1,0:T(8,128)S(1)}, u32[]{:S(2)}, u32[]{:S(2)}) %all-to-all-start.2) | async-done | bytes 524320 | tf_op jit(solution)/shard_map/all_to_all | solution.py:534
  57.4 1.2 %copy-done.2 = bf16[8,8,64,128]{3,2,1,0:T(8,128)(2,1)S(1)} copy-done((bf16[8,8,64,128]{3,2,1,0:T(8,128)(2,1)S(1)}, bf16[8,8,64,128]{3,2,1,0:T(8,128)(2,1)}, u32[]{:S(2)}) %copy-start.2) | copy-done | bytes 1048600
  58.7 0.9 %finish.1 = f32[8,64,128]{2,1,0:T(8,128)S(1)} custom-call(s32[1]{0:T(128)} %bitcast.e_ref, f32[8,32,512]{2,1,0:T(8,128)S(1)} %all-to-all-done.2.r_ref, bf16[128,1024]{1,0:T(8,128)(2,1)S(1)} %get-tuple-element.31.w_ref, bf16[8,8,64,128]{3,2,1,0:T(8,128)(2,1)S(1)} %copy-done.2, f32[8,64,128]{2,1,0:T(8,128)S(1)} %get-tuple-element.36.part_ref), custom_call_target="tpu_custom_call" | custom-call | tf_op jit(solution)/shard_map/finish/pallas_call | solution.py:511
  59.6 4.1 %collective-permute-start = (f32[8,64,128]{2,1,0:T(8,128)S(1)}, f32[8,64,128]{2,1,0:T(8,128)S(1)}, u32[]{:S(2)}, u32[]{:S(2)}) collective-permute-start(f32[8,64,128]{2,1,0:T(8,128)S(1)} %finish.1), channel_id=1, source_target_pairs={{0,1},{1,0},{2,3},{3,2},{4,5},{5,4},{6,7},{7,6},{8,9},{9,8},{10,11... | collective-permute-start | bytes 786440 | tf_op jit(solution)/shard_map/ppermute | solution.py:537
  63.7 1.2 %collective-permute-done = f32[8,64,128]{2,1,0:T(8,128)S(1)} collective-permute-done((f32[8,64,128]{2,1,0:T(8,128)S(1)}, f32[8,64,128]{2,1,0:T(8,128)S(1)}, u32[]{:S(2)}, u32[]{:S(2)}) %collective-permute-start) | collective-permute-done | bytes 262176 | tf_op jit(solution)/shard_map/ppermute | solution.py:537
  64.9 0.7 %add.3 = f32[8,64,128]{2,1,0:T(8,128)} add(f32[8,64,128]{2,1,0:T(8,128)S(1)} %finish.1, f32[8,64,128]{2,1,0:T(8,128)S(1)} %collective-permute-done) | non-fusion elementwise | flops 65536 | bytes 786432 | tf_op jit(solution)/shard_map/add | solution.py:537
  (4 shorter events, 0.0 us)
Async XLA Ops:
  0.0 11.6 %copy-start.7 = (f32[5]{0:T(128)S(1)}, f32[5]{0:T(128)}, u32[]{:S(2)}) copy-start(f32[5]{0:T(128)} %taps_ref.3) | copy-start | bytes 64
  0.0 11.6 %copy-start.6 = (f32[5,8,1024]{2,1,0:T(8,128)S(1)}, f32[5,8,1024]{2,1,0:T(8,128)}, u32[]{:S(2)}) copy-start(f32[5,8,1024]{2,1,0:T(8,128)} %ef_ref.1) | copy-start | bytes 491524
  4.0 16.1 %all-to-all-start = ((f32[16,40,128]{2,1,0:T(8,128)}), f32[16,40,128]{2,1,0:T(8,128)S(1)}, u32[]{:S(2)}, u32[]{:S(2)}) async-start(f32[16,40,128]{2,1,0:T(8,128)} %get-tuple-element.21), calls=%async_computation | async-start | bytes 655360 | tf_op jit(solution)/shard_map/all_to_all | solution.py:526
  11.6 13.5 %copy-start = (f32[8,8,64,128]{3,2,1,0:T(8,128)S(1)}, f32[8,8,64,128]{3,2,1,0:T(8,128)}, u32[]{:S(2)}) copy-start(f32[8,8,64,128]{3,2,1,0:T(8,128)} %alpha_hbm.5) | copy-start | bytes 6291460
  16.7 0.8 %copy-start.8 = (bf16[8,256,128]{2,1,0:T(8,128)(2,1)}, bf16[8,256,128]{2,1,0:T(8,128)(2,1)S(1)}, u32[]{:S(2)}) copy-start(bf16[8,256,128]{2,1,0:T(8,128)(2,1)S(1)} %get-tuple-element.34.e_ref) | copy-start | bytes 1572868
  21.1 11.6 %all-to-all-start.1 = ((f32[16,32,128]{2,1,0:T(8,128)}), f32[16,32,128]{2,1,0:T(8,128)S(1)}, u32[]{:S(2)}, u32[]{:S(2)}) async-start(f32[16,32,128]{2,1,0:T(8,128)} %chain_slabs.1), calls=%async_computation.1 | async-start | bytes 524288 | tf_op jit(solution)/shard_map/all_to_all | solution.py:530
  25.2 1.0 %copy-start.4 = (f32[64,8,128]{2,1,0:T(8,128)S(1)}, f32[64,8,128]{2,1,0:T(8,128)}, u32[]{:S(2)}) copy-start(f32[64,8,128]{2,1,0:T(8,128)} %get-tuple-element.25.s_ref.slab_ref) | copy-start | bytes 786436
  34.8 22.6 %all-to-all-start.2 = ((f32[8,32,512]{2,1,0:T(8,128)}), f32[8,32,512]{2,1,0:T(8,128)S(1)}, u32[]{:S(2)}, u32[]{:S(2)}) async-start(f32[8,32,512]{2,1,0:T(8,128)} %north_finish.1), calls=%async_computation.2 | async-start | bytes 1048576 | tf_op jit(solution)/shard_map/all_to_all | solution.py:534
  43.0 1.2 %copy-start.3 = (bf16[8,8,64,128]{3,2,1,0:T(8,128)(2,1)S(1)}, bf16[8,8,64,128]{3,2,1,0:T(8,128)(2,1)}, u32[]{:S(2)}) copy-start(bf16[8,8,64,128]{3,2,1,0:T(8,128)(2,1)} %pert_ref.1) | copy-start | bytes 3145732
  44.2 0.9 %copy-start.5 = (f32[64,8,128]{2,1,0:T(8,128)S(1)}, f32[64,8,128]{2,1,0:T(8,128)}, u32[]{:S(2)}) copy-start(f32[64,8,128]{2,1,0:T(8,128)} %get-tuple-element.25.s_ref.slab_ref) | copy-start | bytes 786436
  45.2 1.0 %copy-start.9 = (bf16[8,256,128]{2,1,0:T(8,128)(2,1)S(1)}, bf16[8,256,128]{2,1,0:T(8,128)(2,1)}, u32[]{:S(2)}) copy-start(bf16[8,256,128]{2,1,0:T(8,128)(2,1)} %copy-done.8) | copy-start | bytes 1572868
  49.5 1.0 %copy-start.1 = (bf16[8,8,64,128]{3,2,1,0:T(8,128)(2,1)}, bf16[8,8,64,128]{3,2,1,0:T(8,128)(2,1)S(1)}, u32[]{:S(2)}) copy-start(bf16[8,8,64,128]{3,2,1,0:T(8,128)(2,1)S(1)} %get-tuple-element.35.pert_ref) | copy-start | bytes 3145732
  57.4 1.2 %copy-start.2 = (bf16[8,8,64,128]{3,2,1,0:T(8,128)(2,1)S(1)}, bf16[8,8,64,128]{3,2,1,0:T(8,128)(2,1)}, u32[]{:S(2)}) copy-start(bf16[8,8,64,128]{3,2,1,0:T(8,128)(2,1)} %copy-done.1) | copy-start | bytes 3145732
  59.6 5.3 %collective-permute-start = (f32[8,64,128]{2,1,0:T(8,128)S(1)}, f32[8,64,128]{2,1,0:T(8,128)S(1)}, u32[]{:S(2)}, u32[]{:S(2)}) collective-permute-start(f32[8,64,128]{2,1,0:T(8,128)S(1)} %finish.1), channel_id=1, source_target_pairs={{0,1},{1,0},{2,3},{3,2},{4,5},{5,4},{6,7},{7,6},{8,9},{9,8},{10,11... | collective-permute-start | bytes 786440 | tf_op jit(solution)/shard_map/ppermute | solution.py:537
where the time goes:
time: 66.2 us; the launch traced here: 65.6 us
  starting transfers between devices  23.9 us (36%)
  Pallas kernels  18.8 us (28%)
  waiting for transfers between devices  14.8 us (22%)
  local copies, waits for them, and re-layouts  7.16 us (11%)
  other arithmetic  0.73 us (1%)
    all_to_all x1, starting transfers between devices, local(): crossed = lax.all_to_all(crossing, 'east', 0, 0)  8.2 us
    all_to_all x1, starting transfers between devices, local(): gathered = lax.all_to_all(functionals, 'north', 0, 0)  7.6 us
    unnamed x20, local copies, waits for them, and re-layouts  7.16 us
    all_to_all x1, waiting for transfers between devices, local(): crossed = lax.all_to_all(crossing, 'east', 0, 0)  6.94 us
    pallas_call x1, Pallas kernels, east_matrices(): pl.pallas_call(kernel, in_specs=[SMEM, SMEM, VMEM], out_specs=[VMEM, VMEM...  5.01 us
    all_to_all x1, waiting for transfers between devices, local(): lax.all_to_all(chained, 'north', 0, 0).reshape(levels, 8 * members, width)  4.11 us
    ppermute x1, starting transfers between devices, local(): return increment + lax.ppermute(increment, 'group', [(0, 1), (1, 0)])  4.09 us
    all_to_all x1, starting transfers between devices, local(): lax.all_to_all(chained, 'north', 0, 0).reshape(levels, 8 * members, width)  4.02 us
  transfers between devices with their start and end apart: 4, of which 4 were waited for; matrix products, arithmetic and copies ran while one was open for 0% of the time, Pallas kernels for 16%

commit v1 on v0

--- a/solution.py
+++ b/solution.py
@@ -62,9 +62,9 @@
         fetches = copies(alpha_hbm, alpha_ref, sems, members)
         stores = copies(p_ref, p_hbm, p_sems, 2 * levels)
         slab_store = pltpu.make_async_copy(s_ref, s_hbm, s_sem)
-        table_fetch.wait()
         for fetch in fetches:
             fetch.start()
+        table_fetch.wait()
         lane = lanes_of()
         table = [nf_ref[j] for j in range(5)]
         gain = jnp.concatenate([jnp.zeros((levels, 64), F32), table[0]], axis=1)
@@ -477,7 +477,7 @@
             pltpu.VMEM((levels, members * rows, width), F32),
             pltpu.SemaphoreType.DMA((members,)),
         ],
-        compiler_params=pltpu.CompilerParams(vmem_limit_bytes=24 * MIB),
+        compiler_params=pltpu.CompilerParams(vmem_limit_bytes=51 * MIB),
         cost_estimate=pl.CostEstimate(flops=2_000_000_000, bytes_accessed=4 * MIB, transcendentals=0),
         name="own_increment",
     )(taps, alpha, slab, columns, entered, east, perturbations)

time: 66.2 us -> 64.4 us (0.973)
  local copies, waits for them, and re-layouts: 7.16 us -> 1.75 us
  waiting for transfers between devices: 14.8 us -> 17 us
  Pallas kernels: 18.8 us -> 20.4 us
    unnamed x20 -> x14, local copies, waits for them, and re-layouts: 7.16 us -> 1.75 us
    all_to_all x1, waiting for transfers between devices: 6.94 us -> 9.08 us  [local(): crossed = lax.all_to_all(crossing, 'east', 0, 0)]
    pallas_call x1, Pallas kernels: 3.29 us -> 5.34 us  [own_increment(): pl.pallas_call(kernel, in_specs=[SMEM, HBM] + [VMEM] * 5, out_specs=[VMEM...]
  transfers between devices with their start and end apart: 4 -> 4, of which waited for: 4 -> 4; matrix products, arithmetic and copies ran while one was open for 0% -> 0% of each run, Pallas kernels for 16% -> 20%
where the time goes in v1:
time: 64.4 us; the launch traced here: 63.9 us
  starting transfers between devices  23.9 us (37%)
  Pallas kernels  20.4 us (32%)
  waiting for transfers between devices  17 us (26%)
  local copies, waits for them, and re-layouts  1.75 us (3%)
  other arithmetic  0.73 us (1%)
    all_to_all x1, waiting for transfers between devices, local(): crossed = lax.all_to_all(crossing, 'east', 0, 0)  9.08 us
    all_to_all x1, starting transfers between devices, local(): crossed = lax.all_to_all(crossing, 'east', 0, 0)  8.2 us
    all_to_all x1, starting transfers between devices, local(): gathered = lax.all_to_all(functionals, 'north', 0, 0)  7.6 us
    pallas_call x1, Pallas kernels, own_increment(): pl.pallas_call(kernel, in_specs=[SMEM, HBM] + [VMEM] * 5, out_specs=[VMEM...  5.34 us
    pallas_call x1, Pallas kernels, east_matrices(): pl.pallas_call(kernel, in_specs=[SMEM, SMEM, VMEM], out_specs=[VMEM, VMEM...  5.01 us
    ppermute x1, starting transfers between devices, local(): return increment + lax.ppermute(increment, 'group', [(0, 1), (1, 0)])  4.09 us
    all_to_all x1, waiting for transfers between devices, local(): lax.all_to_all(chained, 'north', 0, 0).reshape(levels, 8 * members, width)  4.09 us
    all_to_all x1, starting transfers between devices, local(): lax.all_to_all(chained, 'north', 0, 0).reshape(levels, 8 * members, width)  4.02 us
  transfers between devices with their start and end apart: 4, of which 4 were waited for; matrix products, arithmetic and copies ran while one was open for 0% of the time, Pallas kernels for 20%

profile of v1, /device:TPU:1, one launch (start us, length us, event | category | flops | bytes accessed | tf_op | source)
XLA Modules:
  0.0 63.9 jit_solution(10492121335019983097)
XLA Ops:
  0.0 0.0 copy-start.4
  0.0 0.0 copy-start.3
  0.0 3.5 %north_functionals.1 = (f32[16,40,128]{2,1,0:T(8,128)}, f32[64,8,128]{2,1,0:T(8,128)}) custom-call(f32[5,8,64]{2,1,0:T(8,128)} %nf_hbm.1, f32[8,8,64,128]{3,2,1,0:T(8,128)} %alpha_hbm.5), custom_call_target="tpu_custom_call" | custom-call | tf_op jit(solution)/shard_map/north_functionals/pallas_call | solution.py:112
  3.6 7.6 %all-to-all-start = ((f32[16,40,128]{2,1,0:T(8,128)}), f32[16,40,128]{2,1,0:T(8,128)S(1)}, u32[]{:S(2)}, u32[]{:S(2)}) async-start(f32[16,40,128]{2,1,0:T(8,128)} %get-tuple-element.21), calls=%async_computation | async-start | bytes 655360 | tf_op jit(solution)/shard_map/all_to_all | solution.py:526
  11.2 0.0 copy-done.4
  11.2 0.0 copy-done.3
  11.2 0.0 copy-start
  11.2 5.0 %east_matrices.1 = (bf16[8,256,128]{2,1,0:T(8,128)(2,1)S(1)}, bf16[8,64,128]{2,1,0:T(8,128)(2,1)S(1)}, bf16[128,1024]{1,0:T(8,128)(2,1)S(1)}) custom-call(s32[1]{0:T(128)} %bitcast.e_ref, f32[5]{0:T(128)S(1)} %copy-done.4, f32[5,8,1024]{2,1,0:T(8,128)S(1)} %copy-done.3), custom_call_target="tpu_custom_call" | custom-call | flops 2000000000 | bytes 4194304 | tf_op jit(solution)/shard_map/east_matrices/pallas_call | solution.py:362
  16.2 0.0 copy-start.5
  16.2 0.8 %copy-done.5 = bf16[8,256,128]{2,1,0:T(8,128)(2,1)} copy-done((bf16[8,256,128]{2,1,0:T(8,128)(2,1)}, bf16[8,256,128]{2,1,0:T(8,128)(2,1)S(1)}, u32[]{:S(2)}) %copy-start.5) | copy-done | bytes 524312
  17.0 2.6 %all-to-all-done.r_ref = f32[16,40,128]{2,1,0:T(8,128)S(1)} async-done(((f32[16,40,128]{2,1,0:T(8,128)}), f32[16,40,128]{2,1,0:T(8,128)S(1)}, u32[]{:S(2)}, u32[]{:S(2)}) %all-to-all-start) | async-done | bytes 327712 | tf_op jit(solution)/shard_map/all_to_all | solution.py:526
  19.6 1.0 %chain_slabs.1 = f32[16,32,128]{2,1,0:T(8,128)} custom-call(f32[16,40,128]{2,1,0:T(8,128)S(1)} %all-to-all-done.r_ref), custom_call_target="tpu_custom_call" | custom-call | tf_op jit(solution)/shard_map/chain_slabs/pallas_call | solution.py:164
  20.7 4.0 %all-to-all-start.1 = ((f32[16,32,128]{2,1,0:T(8,128)}), f32[16,32,128]{2,1,0:T(8,128)S(1)}, u32[]{:S(2)}, u32[]{:S(2)}) async-start(f32[16,32,128]{2,1,0:T(8,128)} %chain_slabs.1), calls=%async_computation.1 | async-start | bytes 524288 | tf_op jit(solution)/shard_map/all_to_all | solution.py:530
  24.7 0.0 copy-done
  24.7 0.0 copy-start.1
  24.7 0.9 %copy-done.1 = f32[64,8,128]{2,1,0:T(8,128)S(1)} copy-done((f32[64,8,128]{2,1,0:T(8,128)S(1)}, f32[64,8,128]{2,1,0:T(8,128)}, u32[]{:S(2)}) %copy-start.1) | copy-done | bytes 262168
  25.7 2.5 %own_crossing.1 = (f32[8,32,512]{2,1,0:T(8,128)S(1)}, bf16[8,64,32]{2,1,0:T(8,128)(2,1)S(1)}, bf16[8,32,128]{2,1,0:T(8,128)(2,1)S(1)}) custom-call(f32[8,8,64,128]{3,2,1,0:T(8,128)S(1)} %copy-done, f32[64,8,128]{2,1,0:T(8,128)S(1)} %copy-done.1, bf16[8,64,128]{2,1,0:T(8,128)(2,1)S(1)} %get-tuple-element.26.v_ref), custom_call_target="tpu_custom_call" | custom-call | flops 2000000000 | bytes 4194304 | tf_op jit(solution)/shard_map/own_crossing/pallas_call | solution.py:229
  28.1 0.0 copy-start.2
  28.1 0.0 copy-start.6
  28.1 4.1 %all-to-all-done.1 = f32[16,32,128]{2,1,0:T(8,128)S(1)} async-done(((f32[16,32,128]{2,1,0:T(8,128)}), f32[16,32,128]{2,1,0:T(8,128)S(1)}, u32[]{:S(2)}, u32[]{:S(2)}) %all-to-all-start.1) | async-done | bytes 262176 | tf_op jit(solution)/shard_map/all_to_all | solution.py:530
  32.2 2.1 %north_finish.1 = f32[8,32,512]{2,1,0:T(8,128)} custom-call(f32[8,32,512]{2,1,0:T(8,128)S(1)} %get-tuple-element.27.c0_ref, bf16[8,32,128]{2,1,0:T(8,128)(2,1)S(1)} %get-tuple-element.28.b_ref, f32[8,64,128]{2,1,0:T(8,128)S(1)} %bitcast.2, bf16[8,64,128]{2,1,0:T(8,128)(2,1)S(1)} %get-tuple-element.26.v_ref), custom_call_target="tpu_custom_call" | custom-call | tf_op jit(solution)/shard_map/north_finish/pallas_call | solution.py:424
  34.3 8.2 %all-to-all-start.2 = ((f32[8,32,512]{2,1,0:T(8,128)}), f32[8,32,512]{2,1,0:T(8,128)S(1)}, u32[]{:S(2)}, u32[]{:S(2)}) async-start(f32[8,32,512]{2,1,0:T(8,128)} %north_finish.1), calls=%async_computation.2 | async-start | bytes 1048576 | tf_op jit(solution)/shard_map/all_to_all | solution.py:534
  42.5 0.0 copy-done.2
  42.5 0.0 copy-done.6
  42.5 5.3 %own_increment.1 = (f32[8,64,128]{2,1,0:T(8,128)S(1)}, bf16[8,8,64,128]{3,2,1,0:T(8,128)(2,1)S(1)}) custom-call(f32[5]{0:T(128)S(1)} %copy-done.4, f32[8,8,64,128]{3,2,1,0:T(8,128)} %alpha_hbm.5, f32[64,8,128]{2,1,0:T(8,128)S(1)} %copy-done.2, bf16[8,64,32]{2,1,0:T(8,128)(2,1)S(1)} %get-tuple-element.32.u_ref, f32[8,64,128]{2,1,0:T(8,128)S(1)} %bitcast.3, ...), custom_call_target="tpu_custom_call" | custom-call | flops 2000000000 | bytes 4194304 | tf_op jit(solution)/shard_map/own_increment/pallas_call | solution.py:467
  47.9 9.1 %all-to-all-done.2.r_ref = f32[8,32,512]{2,1,0:T(8,128)S(1)} async-done(((f32[8,32,512]{2,1,0:T(8,128)}), f32[8,32,512]{2,1,0:T(8,128)S(1)}, u32[]{:S(2)}, u32[]{:S(2)}) %all-to-all-start.2) | async-done | bytes 524320 | tf_op jit(solution)/shard_map/all_to_all | solution.py:534
  57.0 0.9 %finish.1 = f32[8,64,128]{2,1,0:T(8,128)S(1)} custom-call(s32[1]{0:T(128)} %bitcast.e_ref, f32[8,32,512]{2,1,0:T(8,128)S(1)} %all-to-all-done.2.r_ref, bf16[128,1024]{1,0:T(8,128)(2,1)S(1)} %get-tuple-element.31.w_ref, bf16[8,8,64,128]{3,2,1,0:T(8,128)(2,1)S(1)} %get-tuple-element.35.pert_ref, f32[8,64,128]{2,1,0:T(8,128)S(1)} %get-tuple-element.36.part_ref), custom_call_target="tpu_custom_call" | custom-call | tf_op jit(solution)/shard_map/finish/pallas_call | solution.py:511
  57.9 4.1 %collective-permute-start = (f32[8,64,128]{2,1,0:T(8,128)S(1)}, f32[8,64,128]{2,1,0:T(8,128)S(1)}, u32[]{:S(2)}, u32[]{:S(2)}) collective-permute-start(f32[8,64,128]{2,1,0:T(8,128)S(1)} %finish.1), channel_id=1, source_target_pairs={{0,1},{1,0},{2,3},{3,2},{4,5},{5,4},{6,7},{7,6},{8,9},{9,8},{10,11... | collective-permute-start | bytes 786440 | tf_op jit(solution)/shard_map/ppermute | solution.py:537
  62.0 1.2 %collective-permute-done = f32[8,64,128]{2,1,0:T(8,128)S(1)} collective-permute-done((f32[8,64,128]{2,1,0:T(8,128)S(1)}, f32[8,64,128]{2,1,0:T(8,128)S(1)}, u32[]{:S(2)}, u32[]{:S(2)}) %collective-permute-start) | collective-permute-done | bytes 262176 | tf_op jit(solution)/shard_map/ppermute | solution.py:537
  63.2 0.7 %add.3 = f32[8,64,128]{2,1,0:T(8,128)} add(f32[8,64,128]{2,1,0:T(8,128)S(1)} %finish.1, f32[8,64,128]{2,1,0:T(8,128)S(1)} %collective-permute-done) | non-fusion elementwise | flops 65536 | bytes 786432 | tf_op jit(solution)/shard_map/add | solution.py:537
Async XLA Ops:
  0.0 11.2 %copy-start.4 = (f32[5]{0:T(128)S(1)}, f32[5]{0:T(128)}, u32[]{:S(2)}) copy-start(f32[5]{0:T(128)} %taps_ref.3) | copy-start | bytes 64
  0.0 11.2 %copy-start.3 = (f32[5,8,1024]{2,1,0:T(8,128)S(1)}, f32[5,8,1024]{2,1,0:T(8,128)}, u32[]{:S(2)}) copy-start(f32[5,8,1024]{2,1,0:T(8,128)} %ef_ref.1) | copy-start | bytes 491524
  3.6 16.1 %all-to-all-start = ((f32[16,40,128]{2,1,0:T(8,128)}), f32[16,40,128]{2,1,0:T(8,128)S(1)}, u32[]{:S(2)}, u32[]{:S(2)}) async-start(f32[16,40,128]{2,1,0:T(8,128)} %get-tuple-element.21), calls=%async_computation | async-start | bytes 655360 | tf_op jit(solution)/shard_map/all_to_all | solution.py:526
  11.2 13.5 %copy-start = (f32[8,8,64,128]{3,2,1,0:T(8,128)S(1)}, f32[8,8,64,128]{3,2,1,0:T(8,128)}, u32[]{:S(2)}) copy-start(f32[8,8,64,128]{3,2,1,0:T(8,128)} %alpha_hbm.5) | copy-start | bytes 6291460
  16.2 0.8 %copy-start.5 = (bf16[8,256,128]{2,1,0:T(8,128)(2,1)}, bf16[8,256,128]{2,1,0:T(8,128)(2,1)S(1)}, u32[]{:S(2)}) copy-start(bf16[8,256,128]{2,1,0:T(8,128)(2,1)S(1)} %get-tuple-element.34.e_ref) | copy-start | bytes 1572868
  20.7 11.6 %all-to-all-start.1 = ((f32[16,32,128]{2,1,0:T(8,128)}), f32[16,32,128]{2,1,0:T(8,128)S(1)}, u32[]{:S(2)}, u32[]{:S(2)}) async-start(f32[16,32,128]{2,1,0:T(8,128)} %chain_slabs.1), calls=%async_computation.1 | async-start | bytes 524288 | tf_op jit(solution)/shard_map/all_to_all | solution.py:530
  24.7 1.0 %copy-start.1 = (f32[64,8,128]{2,1,0:T(8,128)S(1)}, f32[64,8,128]{2,1,0:T(8,128)}, u32[]{:S(2)}) copy-start(f32[64,8,128]{2,1,0:T(8,128)} %get-tuple-element.25.s_ref.slab_ref) | copy-start | bytes 786436
  28.1 14.4 %copy-start.2 = (f32[64,8,128]{2,1,0:T(8,128)S(1)}, f32[64,8,128]{2,1,0:T(8,128)}, u32[]{:S(2)}) copy-start(f32[64,8,128]{2,1,0:T(8,128)} %get-tuple-element.25.s_ref.slab_ref) | copy-start | bytes 786436
  28.1 14.4 %copy-start.6 = (bf16[8,256,128]{2,1,0:T(8,128)(2,1)S(1)}, bf16[8,256,128]{2,1,0:T(8,128)(2,1)}, u32[]{:S(2)}) copy-start(bf16[8,256,128]{2,1,0:T(8,128)(2,1)} %copy-done.5) | copy-start | bytes 1572868
  34.3 22.6 %all-to-all-start.2 = ((f32[8,32,512]{2,1,0:T(8,128)}), f32[8,32,512]{2,1,0:T(8,128)S(1)}, u32[]{:S(2)}, u32[]{:S(2)}) async-start(f32[8,32,512]{2,1,0:T(8,128)} %north_finish.1), calls=%async_computation.2 | async-start | bytes 1048576 | tf_op jit(solution)/shard_map/all_to_all | solution.py:534
  57.9 5.3 %collective-permute-start = (f32[8,64,128]{2,1,0:T(8,128)S(1)}, f32[8,64,128]{2,1,0:T(8,128)S(1)}, u32[]{:S(2)}, u32[]{:S(2)}) collective-permute-start(f32[8,64,128]{2,1,0:T(8,128)S(1)} %finish.1), channel_id=1, source_target_pairs={{0,1},{1,0},{2,3},{3,2},{4,5},{5,4},{6,7},{7,6},{8,9},{9,8},{10,11... | collective-permute-start | bytes 786440 | tf_op jit(solution)/shard_map/ppermute | solution.py:537

commit v2 on v1

--- a/solution.py
+++ b/solution.py
@@ -55,7 +55,7 @@
 
 def north_functionals(levels, members, rows):
     def kernel(
-        nf_hbm, alpha_hbm, p_hbm, s_hbm, nf_ref, alpha_ref, f_ref, s_ref, p_ref, nf_sem, s_sem, sems, p_sems
+        nf_hbm, alpha_hbm, p_hbm, s_hbm, nf_ref, alpha_ref, f_ref, s_ref, p_ref, w_ref, nf_sem, s_sem, sems, p_sems
     ):
         table_fetch = pltpu.make_async_copy(nf_hbm, nf_ref, nf_sem)
         table_fetch.start()
@@ -72,7 +72,9 @@
         for i in range(rows):
             value = jnp.where(lane == 64 + i, gain, 0.0)
             for j in (4, 3, 2, 1):
-                value = value + wide(table[j][:, i : i + 1]) * state[j - 1]
+                weight = wide(table[j][:, i : i + 1])
+                w_ref[i, j - 1] = weight
+                value = value + weight * state[j - 1]
             f_ref[i] = value + unit(lane == 4 + rows - 1 - i) if i >= rows - 4 else value
             state = [value] + state[:3]
         state = [jnp.zeros((levels, 128), F32)] * 4
@@ -80,30 +82,33 @@
             value = f_ref[i]
             for j in (4, 3, 2, 1):
                 if i + j < rows:
-                    value = value + wide(table[j][:, i + j : i + j + 1]) * state[j - 1]
+                    value = value + w_ref[i + j, j - 1] * state[j - 1]
             s_ref[i] = value * wide(table[0][:, i : i + 1])
             state = [value] + state[:3]
         slab_store.start()
-        for fetch in fetches:
-            fetch.wait()
+        lefts = []
         for l in range(levels):
             flat = f_ref[:, l, :]
             maps = jnp.dot(
                 flat.T[0:8], flat, precision=lax.Precision.HIGHEST, preferred_element_type=F32
             )
+            p_ref[2 * l, 32:40, :] = maps
+            p_ref[2 * l + 1, 32:40, :] = maps
             edge = s_ref[:, l, :].T[0:8]
             high, low = split_rounded(jnp.concatenate([edge, edge], axis=1))
-            left = jnp.concatenate([high, low], axis=0).astype(BF16)
+            lefts.append(jnp.concatenate([high, low], axis=0).astype(BF16))
+        for fetch in fetches:
+            fetch.wait()
+        for l in range(levels):
             for half in range(2):
                 right = []
                 for m in range(4):
                     a_high, a_low = split(alpha_ref[half * 4 + m, l])
                     right.append(jnp.concatenate([a_high, a_low], axis=0))
-                out = dot(left, jnp.concatenate(right, axis=1))
+                out = dot(lefts[l], jnp.concatenate(right, axis=1))
                 out = out[0:8] + out[8:16]
                 for m in range(4):
                     p_ref[2 * l + half, 8 * m : 8 * m + 8, :] = out[:, 128 * m : 128 * m + 128]
-                p_ref[2 * l + half, 32:40, :] = maps
                 stores[2 * l + half].start()
         for store in stores + [slab_store]:
             store.wait()
@@ -123,6 +128,7 @@
                 pltpu.VMEM((rows, levels, 128), F32),
                 pltpu.VMEM((rows, levels, 128), F32),
                 pltpu.VMEM((2 * levels, 40, 128), F32),
+                pltpu.VMEM((rows, 4, levels, 128), F32),
                 pltpu.SemaphoreType.DMA,
                 pltpu.SemaphoreType.DMA,
                 pltpu.SemaphoreType.DMA((members,)),
@@ -236,7 +242,7 @@
             jax.ShapeDtypeStruct((levels, rows, 32), BF16),
             jax.ShapeDtypeStruct((levels, 32, 128), BF16),
         ],
-        compiler_params=pltpu.CompilerParams(vmem_limit_bytes=16 * MIB),
+        compiler_params=pltpu.CompilerParams(vmem_limit_bytes=51 * MIB),
         cost_estimate=pl.CostEstimate(flops=2_000_000_000, bytes_accessed=4 * MIB, transcendentals=0),
         name="own_crossing",
     )(alpha, slab, sends)
@@ -247,7 +253,7 @@
     length = 128
     slabs = east_filter.shape[2] // length
 
-    def kernel(e_ref, taps_ref, ef_ref, e_out, v_out, w_out, wt_ref, rt_ref, f_ref, s_ref):
+    def kernel(e_ref, taps_ref, ef_ref, e_out, v_out, w_out, wt_ref, rt_ref, f_ref, s_ref, near_ref):
         me = e_ref[0]
         lane = lanes_of()
         row = rows_of()
@@ -284,6 +290,8 @@
         side = [unit(lane == k) for k in range(4)]
         for i in range(length):
             weight = [wide(own[j][:, i : i + 1]) for j in range(1, 5)]
+            for j in range(4):
+                near_ref[i, j] = weight[j]
             c_value = jnp.where(lane == i, own[0], 0.0)
             s_value = jnp.zeros((levels, 128), F32)
             for j in (3, 2, 1, 0):
@@ -308,7 +316,7 @@
             s_value = f_ref[i, :, 128:256]
             for j in (4, 3, 2, 1):
                 if i + j < length:
-                    weight = wide(own[j][:, i + j : i + j + 1])
+                    weight = near_ref[i + j, j - 1]
                     c_value = c_value + weight * core[j - 1]
                     s_value = s_value + weight * side[j - 1]
             gain = wide(own[0][:, i : i + 1])
@@ -321,35 +329,31 @@
         ]
         entering, pending = [], []
         for l in range(levels):
-            e_high, e_low = split(s_ref[:, l, 0:128])
-            e_out[l] = jnp.concatenate([e_high, e_low], axis=0)
+            e_out[l] = jnp.concatenate(split(s_ref[:, l, 0:128]), axis=0)
             edge = s_ref[:, l, 128:256].T[0:8]
-            start, end = edge[0:4], edge[4:8]
-            entering.append(start)
-            pending.append(end)
-            upward = [end]
-            for e in range(1, slabs):
-                at = 8 * (e - 1) + l
-                moved = sum(
-                    wide(across[j][:, at : at + 1]) * jnp.broadcast_to(upward[-1][j : j + 1], (4, 128))
-                    for j in range(4)
-                )
-                upward.append(jnp.where(e - 1 > me, moved, end))
-            downward = [start]
-            for e in reversed(range(slabs - 1)):
-                at = 8 * (e + 1) + l
-                moved = sum(
-                    wide(step[j][0:4, at : at + 1])
-                    * jnp.broadcast_to(downward[-1][j : j + 1], (4, 128))
-                    for j in range(4)
-                )
-                downward.append(jnp.where(e + 1 < me, moved, start))
-            downward.reverse()
+            entering.append(edge[0:4])
+            pending.append(edge[4:8])
+        upward, downward = [pending], [entering]
+        for e in range(1, slabs):
+            for chain, column, at, beyond, first in (
+                (upward, across, e - 1, e - 1 > me, pending),
+                (downward, step, slabs - e, slabs - e < me, entering),
+            ):
+                moved = [
+                    sum(
+                        wide(column[j][0:4, 8 * at + l : 8 * at + l + 1])
+                        * jnp.broadcast_to(chain[-1][l][j : j + 1], (4, 128))
+                        for j in range(4)
+                    )
+                    for l in range(levels)
+                ]
+                chain.append([jnp.where(beyond, moved[l], first[l]) for l in range(levels)])
+        downward.reverse()
+        for l in range(levels):
             sends = jnp.concatenate(
-                [jnp.where(e > me, upward[e], downward[e]) for e in range(slabs)], axis=0
+                [jnp.where(e > me, upward[e][l], downward[e][l]) for e in range(slabs)], axis=0
             )
-            high, low = split_rounded(sends)
-            v_out[l] = jnp.concatenate([high, low], axis=0).astype(BF16)
+            v_out[l] = jnp.concatenate(split_rounded(sends), axis=0).astype(BF16)
         columns = jnp.concatenate(entering + pending, axis=0)
         level = lax.rem(rows_of(64), 32) // 4
         for k in range(levels):
@@ -373,6 +377,7 @@
             pltpu.VMEM((128, 128), F32),
             pltpu.VMEM((length, levels, 256), F32),
             pltpu.VMEM((length, levels, 256), F32),
+            pltpu.VMEM((length, 4, levels, 128), F32),
         ],
         compiler_params=pltpu.CompilerParams(vmem_limit_bytes=16 * MIB),
         cost_estimate=pl.CostEstimate(flops=2_000_000_000, bytes_accessed=4 * MIB, transcendentals=0),
@@ -392,6 +397,7 @@
             for j in range(levels // 2)
         ]
         empty = jnp.zeros((16, 128), BF16)
+        lefts = []
         for l in range(levels):
             values = [
                 jnp.concatenate(split(z_ref[l, 16 * p : 16 * p + 16, :]), axis=1) for p in range(pairs)
@@ -401,7 +407,8 @@
             )
             high, low = split_rounded(out[0:32] + out[32:64])
             left = jnp.where(lanes_of(32) < 64, high, low).astype(BF16)
-            left = jnp.concatenate([left, left], axis=1)
+            lefts.append(jnp.concatenate([left, left], axis=1))
+        for l in range(levels):
             blocks = [
                 jnp.concatenate(
                     [
@@ -412,7 +419,7 @@
                 )
                 for piece in (b_ref[l, 0:16], b_ref[l, 16:32])
             ]
-            out = dot(left, jnp.concatenate([blocks[0], blocks[0], blocks[1], blocks[1]], axis=0))
+            out = dot(lefts[l], jnp.concatenate([blocks[0], blocks[0], blocks[1], blocks[1]], axis=0))
             for e in range(8):
                 at = slice(4 * l, 4 * l + 4)
                 c_ref[e, at, :] = c0_ref[e, at, :] + out[4 * e : 4 * e + 4]

time: 64.4 us -> 63.1 us (0.980)
  local copies, waits for them, and re-layouts: 1.75 us -> 0.01 us
    unnamed x14 -> x6, local copies, waits for them, and re-layouts: 1.75 us -> 0.01 us
    pallas_call x1, Pallas kernels: 2.46 us -> 3.85 us  [own_crossing(): pl.pallas_call(kernel, in_specs=[HBM, VMEM, VMEM], out_specs=[VMEM] * 3,...]
    all_to_all x1, waiting for transfers between devices: 2.63 us -> 3.45 us  [local(): gathered = lax.all_to_all(functionals, 'north', 0, 0)]
    pallas_call x1, Pallas kernels: 2.09 us -> 1.32 us  [north_finish(): pl.pallas_call(kernel, in_specs=[VMEM] * 4, out_specs=HBM, out_shape=jax....]
  transfers between devices with their start and end apart: 4 -> 4, of which waited for: 4 -> 4; matrix products, arithmetic and copies ran while one was open for 0% -> 0% of each run, Pallas kernels for 20% -> 23%
where the time goes in v2:
time: 63.1 us; the launch traced here: 62.7 us
  starting transfers between devices  23.7 us (38%)
  Pallas kernels  21 us (33%)
  waiting for transfers between devices  17.1 us (27%)
  other arithmetic  0.74 us (1%)
    all_to_all x1, waiting for transfers between devices, local(): crossed = lax.all_to_all(crossing, 'east', 0, 0)  8.84 us
    all_to_all x1, starting transfers between devices, local(): crossed = lax.all_to_all(crossing, 'east', 0, 0)  8.2 us
    all_to_all x1, starting transfers between devices, local(): gathered = lax.all_to_all(functionals, 'north', 0, 0)  7.6 us
    pallas_call x1, Pallas kernels, own_increment(): pl.pallas_call(kernel, in_specs=[SMEM, HBM] + [VMEM] * 5, out_specs=[VMEM...  5.35 us
    pallas_call x1, Pallas kernels, east_matrices(): pl.pallas_call(kernel, in_specs=[SMEM, SMEM, VMEM], out_specs=[VMEM, VMEM...  4.98 us
    ppermute x1, starting transfers between devices, local(): return increment + lax.ppermute(increment, 'group', [(0, 1), (1, 0)])  4.33 us
    pallas_call x1, Pallas kernels, own_crossing(): pl.pallas_call(kernel, in_specs=[HBM, VMEM, VMEM], out_specs=[VMEM] * 3,...  3.85 us
    all_to_all x1, waiting for transfers between devices, local(): lax.all_to_all(chained, 'north', 0, 0).reshape(levels, 8 * members, width)  3.69 us
  transfers between devices with their start and end apart: 4, of which 4 were waited for; matrix products, arithmetic and copies ran while one was open for 0% of the time, Pallas kernels for 23%

profile of v2, /device:TPU:1, one launch (start us, length us, event | category | flops | bytes accessed | tf_op | source)
XLA Modules:
  0.0 62.7 jit_solution(8755921496357557495)
XLA Ops:
  0.0 0.0 copy-start.2
  0.0 0.0 copy-start.1
  0.0 3.6 %north_functionals.1 = (f32[16,40,128]{2,1,0:T(8,128)}, f32[64,8,128]{2,1,0:T(8,128)}) custom-call(f32[5,8,64]{2,1,0:T(8,128)} %nf_hbm.1, f32[8,8,64,128]{3,2,1,0:T(8,128)} %alpha_hbm.5), custom_call_target="tpu_custom_call" | custom-call | tf_op jit(solution)/shard_map/north_functionals/pallas_call | solution.py:117
  3.6 7.6 %all-to-all-start = ((f32[16,40,128]{2,1,0:T(8,128)}), f32[16,40,128]{2,1,0:T(8,128)S(1)}, u32[]{:S(2)}, u32[]{:S(2)}) async-start(f32[16,40,128]{2,1,0:T(8,128)} %get-tuple-element.21), calls=%async_computation | async-start | bytes 655360 | tf_op jit(solution)/shard_map/all_to_all | solution.py:533
  11.2 0.0 copy-done.2
  11.2 0.0 copy-done.1
  11.2 0.0 copy-start
  11.2 5.0 %east_matrices.1 = (bf16[8,256,128]{2,1,0:T(8,128)(2,1)S(1)}, bf16[8,64,128]{2,1,0:T(8,128)(2,1)S(1)}, bf16[128,1024]{1,0:T(8,128)(2,1)S(1)}) custom-call(s32[1]{0:T(128)} %bitcast.e_ref, f32[5]{0:T(128)S(1)} %copy-done.2, f32[5,8,1024]{2,1,0:T(8,128)S(1)} %copy-done.1), custom_call_target="tpu_custom_call" | custom-call | flops 2000000000 | bytes 4194304 | tf_op jit(solution)/shard_map/east_matrices/pallas_call | solution.py:366
  16.2 3.5 %all-to-all-done.r_ref = f32[16,40,128]{2,1,0:T(8,128)S(1)} async-done(((f32[16,40,128]{2,1,0:T(8,128)}), f32[16,40,128]{2,1,0:T(8,128)S(1)}, u32[]{:S(2)}, u32[]{:S(2)}) %all-to-all-start) | async-done | bytes 327712 | tf_op jit(solution)/shard_map/all_to_all | solution.py:533
  19.6 1.0 %chain_slabs.1 = f32[16,32,128]{2,1,0:T(8,128)} custom-call(f32[16,40,128]{2,1,0:T(8,128)S(1)} %all-to-all-done.r_ref), custom_call_target="tpu_custom_call" | custom-call | tf_op jit(solution)/shard_map/chain_slabs/pallas_call | solution.py:170
  20.7 3.5 %all-to-all-start.1 = ((f32[16,32,128]{2,1,0:T(8,128)}), f32[16,32,128]{2,1,0:T(8,128)S(1)}, u32[]{:S(2)}, u32[]{:S(2)}) async-start(f32[16,32,128]{2,1,0:T(8,128)} %chain_slabs.1), calls=%async_computation.1 | async-start | bytes 524288 | tf_op jit(solution)/shard_map/all_to_all | solution.py:537
  24.2 0.0 copy-done
  24.2 3.9 %own_crossing.1 = (f32[8,32,512]{2,1,0:T(8,128)S(1)}, bf16[8,64,32]{2,1,0:T(8,128)(2,1)S(1)}, bf16[8,32,128]{2,1,0:T(8,128)(2,1)S(1)}) custom-call(f32[8,8,64,128]{3,2,1,0:T(8,128)} %alpha_hbm.5, f32[64,8,128]{2,1,0:T(8,128)S(1)} %copy-done, bf16[8,64,128]{2,1,0:T(8,128)(2,1)S(1)} %get-tuple-element.26.v_ref), custom_call_target="tpu_custom_call" | custom-call | flops 2000000000 | bytes 4194304 | tf_op jit(solution)/shard_map/own_crossing/pallas_call | solution.py:235
  28.1 3.7 %all-to-all-done.1 = f32[16,32,128]{2,1,0:T(8,128)S(1)} async-done(((f32[16,32,128]{2,1,0:T(8,128)}), f32[16,32,128]{2,1,0:T(8,128)S(1)}, u32[]{:S(2)}, u32[]{:S(2)}) %all-to-all-start.1) | async-done | bytes 262176 | tf_op jit(solution)/shard_map/all_to_all | solution.py:537
  31.8 1.3 %north_finish.1 = f32[8,32,512]{2,1,0:T(8,128)} custom-call(f32[8,32,512]{2,1,0:T(8,128)S(1)} %get-tuple-element.27.c0_ref, bf16[8,32,128]{2,1,0:T(8,128)(2,1)S(1)} %get-tuple-element.28.b_ref, f32[8,64,128]{2,1,0:T(8,128)S(1)} %bitcast.2, bf16[8,64,128]{2,1,0:T(8,128)(2,1)S(1)} %get-tuple-element.26.v_ref), custom_call_target="tpu_custom_call" | custom-call | tf_op jit(solution)/shard_map/north_finish/pallas_call | solution.py:431
  33.1 8.2 %all-to-all-start.2 = ((f32[8,32,512]{2,1,0:T(8,128)}), f32[8,32,512]{2,1,0:T(8,128)S(1)}, u32[]{:S(2)}, u32[]{:S(2)}) async-start(f32[8,32,512]{2,1,0:T(8,128)} %north_finish.1), calls=%async_computation.2 | async-start | bytes 1048576 | tf_op jit(solution)/shard_map/all_to_all | solution.py:541
  41.3 5.4 %own_increment.1 = (f32[8,64,128]{2,1,0:T(8,128)S(1)}, bf16[8,8,64,128]{3,2,1,0:T(8,128)(2,1)S(1)}) custom-call(f32[5]{0:T(128)S(1)} %copy-done.2, f32[8,8,64,128]{3,2,1,0:T(8,128)} %alpha_hbm.5, f32[64,8,128]{2,1,0:T(8,128)S(1)} %copy-done, bf16[8,64,32]{2,1,0:T(8,128)(2,1)S(1)} %get-tuple-element.32.u_ref, f32[8,64,128]{2,1,0:T(8,128)S(1)} %bitcast.3, ...), custom_call_target="tpu_custom_call" | custom-call | flops 2000000000 | bytes 4194304 | tf_op jit(solution)/shard_map/own_increment/pallas_call | solution.py:474
  46.7 8.8 %all-to-all-done.2.r_ref = f32[8,32,512]{2,1,0:T(8,128)S(1)} async-done(((f32[8,32,512]{2,1,0:T(8,128)}), f32[8,32,512]{2,1,0:T(8,128)S(1)}, u32[]{:S(2)}, u32[]{:S(2)}) %all-to-all-start.2) | async-done | bytes 524320 | tf_op jit(solution)/shard_map/all_to_all | solution.py:541
  55.5 0.9 %finish.1 = f32[8,64,128]{2,1,0:T(8,128)S(1)} custom-call(s32[1]{0:T(128)} %bitcast.e_ref, f32[8,32,512]{2,1,0:T(8,128)S(1)} %all-to-all-done.2.r_ref, bf16[128,1024]{1,0:T(8,128)(2,1)S(1)} %get-tuple-element.31.w_ref, bf16[8,8,64,128]{3,2,1,0:T(8,128)(2,1)S(1)} %get-tuple-element.35.pert_ref, f32[8,64,128]{2,1,0:T(8,128)S(1)} %get-tuple-element.36.part_ref), custom_call_target="tpu_custom_call" | custom-call | tf_op jit(solution)/shard_map/finish/pallas_call | solution.py:518
  56.4 4.3 %collective-permute-start = (f32[8,64,128]{2,1,0:T(8,128)S(1)}, f32[8,64,128]{2,1,0:T(8,128)S(1)}, u32[]{:S(2)}, u32[]{:S(2)}) collective-permute-start(f32[8,64,128]{2,1,0:T(8,128)S(1)} %finish.1), channel_id=1, source_target_pairs={{0,1},{1,0},{2,3},{3,2},{4,5},{5,4},{6,7},{7,6},{8,9},{9,8},{10,11... | collective-permute-start | bytes 786440 | tf_op jit(solution)/shard_map/ppermute | solution.py:544
  60.8 1.2 %collective-permute-done = f32[8,64,128]{2,1,0:T(8,128)S(1)} collective-permute-done((f32[8,64,128]{2,1,0:T(8,128)S(1)}, f32[8,64,128]{2,1,0:T(8,128)S(1)}, u32[]{:S(2)}, u32[]{:S(2)}) %collective-permute-start) | collective-permute-done | bytes 262176 | tf_op jit(solution)/shard_map/ppermute | solution.py:544
  61.9 0.7 %add.3 = f32[8,64,128]{2,1,0:T(8,128)} add(f32[8,64,128]{2,1,0:T(8,128)S(1)} %finish.1, f32[8,64,128]{2,1,0:T(8,128)S(1)} %collective-permute-done) | non-fusion elementwise | flops 65536 | bytes 786432 | tf_op jit(solution)/shard_map/add | solution.py:544
Async XLA Ops:
  0.0 11.2 %copy-start.2 = (f32[5]{0:T(128)S(1)}, f32[5]{0:T(128)}, u32[]{:S(2)}) copy-start(f32[5]{0:T(128)} %taps_ref.3) | copy-start | bytes 64
  0.0 11.2 %copy-start.1 = (f32[5,8,1024]{2,1,0:T(8,128)S(1)}, f32[5,8,1024]{2,1,0:T(8,128)}, u32[]{:S(2)}) copy-start(f32[5,8,1024]{2,1,0:T(8,128)} %ef_ref.1) | copy-start | bytes 491524
  3.6 16.1 %all-to-all-start = ((f32[16,40,128]{2,1,0:T(8,128)}), f32[16,40,128]{2,1,0:T(8,128)S(1)}, u32[]{:S(2)}, u32[]{:S(2)}) async-start(f32[16,40,128]{2,1,0:T(8,128)} %get-tuple-element.21), calls=%async_computation | async-start | bytes 655360 | tf_op jit(solution)/shard_map/all_to_all | solution.py:533
  11.2 13.0 %copy-start = (f32[64,8,128]{2,1,0:T(8,128)S(1)}, f32[64,8,128]{2,1,0:T(8,128)}, u32[]{:S(2)}) copy-start(f32[64,8,128]{2,1,0:T(8,128)} %get-tuple-element.25.s_ref.slab_ref) | copy-start | bytes 786436
  20.7 11.1 %all-to-all-start.1 = ((f32[16,32,128]{2,1,0:T(8,128)}), f32[16,32,128]{2,1,0:T(8,128)S(1)}, u32[]{:S(2)}, u32[]{:S(2)}) async-start(f32[16,32,128]{2,1,0:T(8,128)} %chain_slabs.1), calls=%async_computation.1 | async-start | bytes 524288 | tf_op jit(solution)/shard_map/all_to_all | solution.py:537
  33.1 22.4 %all-to-all-start.2 = ((f32[8,32,512]{2,1,0:T(8,128)}), f32[8,32,512]{2,1,0:T(8,128)S(1)}, u32[]{:S(2)}, u32[]{:S(2)}) async-start(f32[8,32,512]{2,1,0:T(8,128)} %north_finish.1), calls=%async_computation.2 | async-start | bytes 1048576 | tf_op jit(solution)/shard_map/all_to_all | solution.py:541
  56.4 5.5 %collective-permute-start = (f32[8,64,128]{2,1,0:T(8,128)S(1)}, f32[8,64,128]{2,1,0:T(8,128)S(1)}, u32[]{:S(2)}, u32[]{:S(2)}) collective-permute-start(f32[8,64,128]{2,1,0:T(8,128)S(1)} %finish.1), channel_id=1, source_target_pairs={{0,1},{1,0},{2,3},{3,2},{4,5},{5,4},{6,7},{7,6},{8,9},{9,8},{10,11... | collective-permute-start | bytes 786440 | tf_op jit(solution)/shard_map/ppermute | solution.py:544

commit v3 on v2

--- a/solution.py
+++ b/solution.py
@@ -55,15 +55,14 @@
 
 def north_functionals(levels, members, rows):
     def kernel(
-        nf_hbm, alpha_hbm, p_hbm, s_hbm, nf_ref, alpha_ref, f_ref, s_ref, p_ref, w_ref, nf_sem, s_sem, sems, p_sems
+        nf_hbm, alpha_hbm, p_hbm, s_hbm, nf_ref, alpha_ref, f_ref, s_ref, p_ref, w_ref, nf_sem, s_sem, sem, p_sems
     ):
         table_fetch = pltpu.make_async_copy(nf_hbm, nf_ref, nf_sem)
         table_fetch.start()
-        fetches = copies(alpha_hbm, alpha_ref, sems, members)
+        fetch = pltpu.make_async_copy(alpha_hbm, alpha_ref, sem)
         stores = copies(p_ref, p_hbm, p_sems, 2 * levels)
         slab_store = pltpu.make_async_copy(s_ref, s_hbm, s_sem)
-        for fetch in fetches:
-            fetch.start()
+        fetch.start()
         table_fetch.wait()
         lane = lanes_of()
         table = [nf_ref[j] for j in range(5)]
@@ -97,8 +96,7 @@
             edge = s_ref[:, l, :].T[0:8]
             high, low = split_rounded(jnp.concatenate([edge, edge], axis=1))
             lefts.append(jnp.concatenate([high, low], axis=0).astype(BF16))
-        for fetch in fetches:
-            fetch.wait()
+        fetch.wait()
         for l in range(levels):
             for half in range(2):
                 right = []
@@ -131,7 +129,7 @@
                 pltpu.VMEM((rows, 4, levels, 128), F32),
                 pltpu.SemaphoreType.DMA,
                 pltpu.SemaphoreType.DMA,
-                pltpu.SemaphoreType.DMA((members,)),
+                pltpu.SemaphoreType.DMA,
                 pltpu.SemaphoreType.DMA((2 * levels,)),
             ],
             compiler_params=pltpu.CompilerParams(vmem_limit_bytes=63 * MIB),
@@ -210,12 +208,10 @@
 def own_crossing(alpha, slab, sends):
     members, levels, rows, width = alpha.shape
 
-    def kernel(alpha_hbm, s_ref, v_ref, c_ref, u_ref, b_ref, alpha_ref, sems):
-        fetches = copies(alpha_hbm, alpha_ref, sems, members)
-        for fetch in fetches:
-            fetch.start()
-        for fetch in fetches:
-            fetch.wait()
+    def kernel(alpha_hbm, s_ref, v_ref, c_ref, u_ref, b_ref, alpha_ref, sem):
+        fetch = pltpu.make_async_copy(alpha_hbm, alpha_ref, sem)
+        fetch.start()
+        fetch.wait()
         lane = lanes_of()
         for l in range(levels):
             full = s_ref[:, l, :]
@@ -236,7 +232,7 @@
         kernel,
         in_specs=[HBM, VMEM, VMEM],
         out_specs=[VMEM] * 3,
-        scratch_shapes=[pltpu.VMEM(alpha.shape, F32), pltpu.SemaphoreType.DMA((members,))],
+        scratch_shapes=[pltpu.VMEM(alpha.shape, F32), pltpu.SemaphoreType.DMA],
         out_shape=[
             jax.ShapeDtypeStruct((8, 4 * levels, members * rows), F32),
             jax.ShapeDtypeStruct((levels, rows, 32), BF16),
@@ -392,9 +388,9 @@
     def kernel(c0_ref, b_ref, z_ref, v_ref, c_hbm, c_ref, sems):
         stores = [
             pltpu.make_async_copy(
-                c_ref.at[:, pl.ds(8 * j, 8)], c_hbm.at[:, pl.ds(8 * j, 8)], sems.at[j]
+                c_ref.at[:, pl.ds(16 * j, 16)], c_hbm.at[:, pl.ds(16 * j, 16)], sems.at[j]
             )
-            for j in range(levels // 2)
+            for j in range(levels // 4)
         ]
         empty = jnp.zeros((16, 128), BF16)
         lefts = []
@@ -423,8 +419,8 @@
             for e in range(8):
                 at = slice(4 * l, 4 * l + 4)
                 c_ref[e, at, :] = c0_ref[e, at, :] + out[4 * e : 4 * e + 4]
-            if l % 2:
-                stores[l // 2].start()
+            if l % 4 == 3:
+                stores[l // 4].start()
         for store in stores:
             store.wait()
 
@@ -433,7 +429,7 @@
         in_specs=[VMEM] * 4,
         out_specs=HBM,
         out_shape=jax.ShapeDtypeStruct(own.shape, F32),
-        scratch_shapes=[pltpu.VMEM(own.shape, F32), pltpu.SemaphoreType.DMA((levels // 2,))],
+        scratch_shapes=[pltpu.VMEM(own.shape, F32), pltpu.SemaphoreType.DMA((levels // 4,))],
         compiler_params=pltpu.CompilerParams(vmem_limit_bytes=16 * MIB),
         name="north_finish",
     )(own, edges, entered, sends)
@@ -442,12 +438,10 @@
 def own_increment(taps, alpha, slab, columns, entered, east, perturbations, scale):
     members, levels, rows, width = alpha.shape
 
-    def kernel(taps_ref, alpha_hbm, slab_ref, u_ref, z_ref, e_ref, pert_ref, out_ref, keep_ref, alpha_ref, s_ref, sems):
-        fetches = copies(alpha_hbm, alpha_ref, sems, members)
-        for fetch in fetches:
-            fetch.start()
-        for fetch in fetches:
-            fetch.wait()
+    def kernel(taps_ref, alpha_hbm, slab_ref, u_ref, z_ref, e_ref, pert_ref, out_ref, keep_ref, alpha_ref, s_ref, sem):
+        fetch = pltpu.make_async_copy(alpha_hbm, alpha_ref, sem)
+        fetch.start()
+        fetch.wait()
         for l in range(levels):
             added = dot(u_ref[l], edge_right(z_ref, l, members))
             for first, out in north_slab(slab_left(slab_ref[:, l, :]), alpha_ref, l, members):
@@ -482,7 +476,7 @@
         scratch_shapes=[
             pltpu.VMEM(alpha.shape, F32),
             pltpu.VMEM((levels, members * rows, width), F32),
-            pltpu.SemaphoreType.DMA((members,)),
+            pltpu.SemaphoreType.DMA,
         ],
         compiler_params=pltpu.CompilerParams(vmem_limit_bytes=51 * MIB),
         cost_estimate=pl.CostEstimate(flops=2_000_000_000, bytes_accessed=4 * MIB, transcendentals=0),

time: 63.1 us -> 62.5 us (level)
  no operation moved by 1% of the time
where the time goes in v3:
time: 62.5 us; the launch traced here: 62.1 us
  starting transfers between devices  23.7 us (38%)
  Pallas kernels  20.4 us (33%)
  waiting for transfers between devices  17.1 us (27%)
  other arithmetic  0.74 us (1%)
    all_to_all x1, waiting for transfers between devices, local(): crossed = lax.all_to_all(crossing, 'east', 0, 0)  8.82 us
    all_to_all x1, starting transfers between devices, local(): crossed = lax.all_to_all(crossing, 'east', 0, 0)  8.2 us
    all_to_all x1, starting transfers between devices, local(): gathered = lax.all_to_all(functionals, 'north', 0, 0)  7.6 us
    pallas_call x1, Pallas kernels, own_increment(): pl.pallas_call(kernel, in_specs=[SMEM, HBM] + [VMEM] * 5, out_specs=[VMEM...  5.38 us
    pallas_call x1, Pallas kernels, east_matrices(): pl.pallas_call(kernel, in_specs=[SMEM, SMEM, VMEM], out_specs=[VMEM, VMEM...  4.98 us
    ppermute x1, starting transfers between devices, local(): return increment + lax.ppermute(increment, 'group', [(0, 1), (1, 0)])  4.33 us
    pallas_call x1, Pallas kernels, own_crossing(): pl.pallas_call(kernel, in_specs=[HBM, VMEM, VMEM], out_specs=[VMEM] * 3,...  3.88 us
    all_to_all x1, waiting for transfers between devices, local(): lax.all_to_all(chained, 'north', 0, 0).reshape(levels, 8 * members, width)  3.67 us
  transfers between devices with their start and end apart: 4, of which 4 were waited for; matrix products, arithmetic and copies ran while one was open for 0% of the time, Pallas kernels for 23%

profile of v3, /device:TPU:1, one launch (start us, length us, event | category | flops | bytes accessed | tf_op | source)
XLA Modules:
  0.0 62.1 jit_solution(17066589573892892279)
XLA Ops:
  0.0 0.0 copy-start.2
  0.0 0.0 copy-start.1
  0.0 2.9 %north_functionals.1 = (f32[16,40,128]{2,1,0:T(8,128)}, f32[64,8,128]{2,1,0:T(8,128)}) custom-call(f32[5,8,64]{2,1,0:T(8,128)} %nf_hbm.1, f32[8,8,64,128]{3,2,1,0:T(8,128)} %alpha_hbm.5), custom_call_target="tpu_custom_call" | custom-call | tf_op jit(solution)/shard_map/north_functionals/pallas_call | solution.py:115
  2.9 7.6 %all-to-all-start = ((f32[16,40,128]{2,1,0:T(8,128)}), f32[16,40,128]{2,1,0:T(8,128)S(1)}, u32[]{:S(2)}, u32[]{:S(2)}) async-start(f32[16,40,128]{2,1,0:T(8,128)} %get-tuple-element.21), calls=%async_computation | async-start | bytes 655360 | tf_op jit(solution)/shard_map/all_to_all | solution.py:527
  10.6 0.0 copy-done.2
  10.6 0.0 copy-done.1
  10.6 0.0 copy-start
  10.6 5.0 %east_matrices.1 = (bf16[8,256,128]{2,1,0:T(8,128)(2,1)S(1)}, bf16[8,64,128]{2,1,0:T(8,128)(2,1)S(1)}, bf16[128,1024]{1,0:T(8,128)(2,1)S(1)}) custom-call(s32[1]{0:T(128)} %bitcast.e_ref, f32[5]{0:T(128)S(1)} %copy-done.2, f32[5,8,1024]{2,1,0:T(8,128)S(1)} %copy-done.1), custom_call_target="tpu_custom_call" | custom-call | flops 2000000000 | bytes 4194304 | tf_op jit(solution)/shard_map/east_matrices/pallas_call | solution.py:362
  15.6 3.5 %all-to-all-done.r_ref = f32[16,40,128]{2,1,0:T(8,128)S(1)} async-done(((f32[16,40,128]{2,1,0:T(8,128)}), f32[16,40,128]{2,1,0:T(8,128)S(1)}, u32[]{:S(2)}, u32[]{:S(2)}) %all-to-all-start) | async-done | bytes 327712 | tf_op jit(solution)/shard_map/all_to_all | solution.py:527
  19.0 1.0 %chain_slabs.1 = f32[16,32,128]{2,1,0:T(8,128)} custom-call(f32[16,40,128]{2,1,0:T(8,128)S(1)} %all-to-all-done.r_ref), custom_call_target="tpu_custom_call" | custom-call | tf_op jit(solution)/shard_map/chain_slabs/pallas_call | solution.py:168
  20.0 3.5 %all-to-all-start.1 = ((f32[16,32,128]{2,1,0:T(8,128)}), f32[16,32,128]{2,1,0:T(8,128)S(1)}, u32[]{:S(2)}, u32[]{:S(2)}) async-start(f32[16,32,128]{2,1,0:T(8,128)} %chain_slabs.1), calls=%async_computation.1 | async-start | bytes 524288 | tf_op jit(solution)/shard_map/all_to_all | solution.py:531
  23.6 0.0 copy-done
  23.6 3.9 %own_crossing.1 = (f32[8,32,512]{2,1,0:T(8,128)S(1)}, bf16[8,64,32]{2,1,0:T(8,128)(2,1)S(1)}, bf16[8,32,128]{2,1,0:T(8,128)(2,1)S(1)}) custom-call(f32[8,8,64,128]{3,2,1,0:T(8,128)} %alpha_hbm.5, f32[64,8,128]{2,1,0:T(8,128)S(1)} %copy-done, bf16[8,64,128]{2,1,0:T(8,128)(2,1)S(1)} %get-tuple-element.26.v_ref), custom_call_target="tpu_custom_call" | custom-call | flops 2000000000 | bytes 4194304 | tf_op jit(solution)/shard_map/own_crossing/pallas_call | solution.py:231
  27.5 3.7 %all-to-all-done.1 = f32[16,32,128]{2,1,0:T(8,128)S(1)} async-done(((f32[16,32,128]{2,1,0:T(8,128)}), f32[16,32,128]{2,1,0:T(8,128)S(1)}, u32[]{:S(2)}, u32[]{:S(2)}) %all-to-all-start.1) | async-done | bytes 262176 | tf_op jit(solution)/shard_map/all_to_all | solution.py:531
  31.2 1.3 %north_finish.1 = f32[8,32,512]{2,1,0:T(8,128)} custom-call(f32[8,32,512]{2,1,0:T(8,128)S(1)} %get-tuple-element.27.c0_ref, bf16[8,32,128]{2,1,0:T(8,128)(2,1)S(1)} %get-tuple-element.28.b_ref, f32[8,64,128]{2,1,0:T(8,128)S(1)} %bitcast.2, bf16[8,64,128]{2,1,0:T(8,128)(2,1)S(1)} %get-tuple-element.26.v_ref), custom_call_target="tpu_custom_call" | custom-call | tf_op jit(solution)/shard_map/north_finish/pallas_call | solution.py:427
  32.5 8.2 %all-to-all-start.2 = ((f32[8,32,512]{2,1,0:T(8,128)}), f32[8,32,512]{2,1,0:T(8,128)S(1)}, u32[]{:S(2)}, u32[]{:S(2)}) async-start(f32[8,32,512]{2,1,0:T(8,128)} %north_finish.1), calls=%async_computation.2 | async-start | bytes 1048576 | tf_op jit(solution)/shard_map/all_to_all | solution.py:535
  40.7 5.4 %own_increment.1 = (f32[8,64,128]{2,1,0:T(8,128)S(1)}, bf16[8,8,64,128]{3,2,1,0:T(8,128)(2,1)S(1)}) custom-call(f32[5]{0:T(128)S(1)} %copy-done.2, f32[8,8,64,128]{3,2,1,0:T(8,128)} %alpha_hbm.5, f32[64,8,128]{2,1,0:T(8,128)S(1)} %copy-done, bf16[8,64,32]{2,1,0:T(8,128)(2,1)S(1)} %get-tuple-element.32.u_ref, f32[8,64,128]{2,1,0:T(8,128)S(1)} %bitcast.3, ...), custom_call_target="tpu_custom_call" | custom-call | flops 2000000000 | bytes 4194304 | tf_op jit(solution)/shard_map/own_increment/pallas_call | solution.py:468
  46.1 8.8 %all-to-all-done.2.r_ref = f32[8,32,512]{2,1,0:T(8,128)S(1)} async-done(((f32[8,32,512]{2,1,0:T(8,128)}), f32[8,32,512]{2,1,0:T(8,128)S(1)}, u32[]{:S(2)}, u32[]{:S(2)}) %all-to-all-start.2) | async-done | bytes 524320 | tf_op jit(solution)/shard_map/all_to_all | solution.py:535
  54.9 0.9 %finish.1 = f32[8,64,128]{2,1,0:T(8,128)S(1)} custom-call(s32[1]{0:T(128)} %bitcast.e_ref, f32[8,32,512]{2,1,0:T(8,128)S(1)} %all-to-all-done.2.r_ref, bf16[128,1024]{1,0:T(8,128)(2,1)S(1)} %get-tuple-element.31.w_ref, bf16[8,8,64,128]{3,2,1,0:T(8,128)(2,1)S(1)} %get-tuple-element.35.pert_ref, f32[8,64,128]{2,1,0:T(8,128)S(1)} %get-tuple-element.36.part_ref), custom_call_target="tpu_custom_call" | custom-call | tf_op jit(solution)/shard_map/finish/pallas_call | solution.py:512
  55.8 4.3 %collective-permute-start = (f32[8,64,128]{2,1,0:T(8,128)S(1)}, f32[8,64,128]{2,1,0:T(8,128)S(1)}, u32[]{:S(2)}, u32[]{:S(2)}) collective-permute-start(f32[8,64,128]{2,1,0:T(8,128)S(1)} %finish.1), channel_id=1, source_target_pairs={{0,1},{1,0},{2,3},{3,2},{4,5},{5,4},{6,7},{7,6},{8,9},{9,8},{10,11... | collective-permute-start | bytes 786440 | tf_op jit(solution)/shard_map/ppermute | solution.py:538
  60.2 1.2 %collective-permute-done = f32[8,64,128]{2,1,0:T(8,128)S(1)} collective-permute-done((f32[8,64,128]{2,1,0:T(8,128)S(1)}, f32[8,64,128]{2,1,0:T(8,128)S(1)}, u32[]{:S(2)}, u32[]{:S(2)}) %collective-permute-start) | collective-permute-done | bytes 262176 | tf_op jit(solution)/shard_map/ppermute | solution.py:538
  61.3 0.7 %add.3 = f32[8,64,128]{2,1,0:T(8,128)} add(f32[8,64,128]{2,1,0:T(8,128)S(1)} %finish.1, f32[8,64,128]{2,1,0:T(8,128)S(1)} %collective-permute-done) | non-fusion elementwise | flops 65536 | bytes 786432 | tf_op jit(solution)/shard_map/add | solution.py:538
Async XLA Ops:
  0.0 10.6 %copy-start.2 = (f32[5]{0:T(128)S(1)}, f32[5]{0:T(128)}, u32[]{:S(2)}) copy-start(f32[5]{0:T(128)} %taps_ref.3) | copy-start | bytes 64
  0.0 10.6 %copy-start.1 = (f32[5,8,1024]{2,1,0:T(8,128)S(1)}, f32[5,8,1024]{2,1,0:T(8,128)}, u32[]{:S(2)}) copy-start(f32[5,8,1024]{2,1,0:T(8,128)} %ef_ref.1) | copy-start | bytes 491524
  2.9 16.1 %all-to-all-start = ((f32[16,40,128]{2,1,0:T(8,128)}), f32[16,40,128]{2,1,0:T(8,128)S(1)}, u32[]{:S(2)}, u32[]{:S(2)}) async-start(f32[16,40,128]{2,1,0:T(8,128)} %get-tuple-element.21), calls=%async_computation | async-start | bytes 655360 | tf_op jit(solution)/shard_map/all_to_all | solution.py:527
  10.6 13.0 %copy-start = (f32[64,8,128]{2,1,0:T(8,128)S(1)}, f32[64,8,128]{2,1,0:T(8,128)}, u32[]{:S(2)}) copy-start(f32[64,8,128]{2,1,0:T(8,128)} %get-tuple-element.25.s_ref.slab_ref) | copy-start | bytes 786436
  20.0 11.1 %all-to-all-start.1 = ((f32[16,32,128]{2,1,0:T(8,128)}), f32[16,32,128]{2,1,0:T(8,128)S(1)}, u32[]{:S(2)}, u32[]{:S(2)}) async-start(f32[16,32,128]{2,1,0:T(8,128)} %chain_slabs.1), calls=%async_computation.1 | async-start | bytes 524288 | tf_op jit(solution)/shard_map/all_to_all | solution.py:531
  32.5 22.4 %all-to-all-start.2 = ((f32[8,32,512]{2,1,0:T(8,128)}), f32[8,32,512]{2,1,0:T(8,128)S(1)}, u32[]{:S(2)}, u32[]{:S(2)}) async-start(f32[8,32,512]{2,1,0:T(8,128)} %north_finish.1), calls=%async_computation.2 | async-start | bytes 1048576 | tf_op jit(solution)/shard_map/all_to_all | solution.py:535
  55.8 5.5 %collective-permute-start = (f32[8,64,128]{2,1,0:T(8,128)S(1)}, f32[8,64,128]{2,1,0:T(8,128)S(1)}, u32[]{:S(2)}, u32[]{:S(2)}) collective-permute-start(f32[8,64,128]{2,1,0:T(8,128)S(1)} %finish.1), channel_id=1, source_target_pairs={{0,1},{1,0},{2,3},{3,2},{4,5},{5,4},{6,7},{7,6},{8,9},{9,8},{10,11... | collective-permute-start | bytes 786440 | tf_op jit(solution)/shard_map/ppermute | solution.py:538

commit v4 on v3

--- a/solution.py
+++ b/solution.py
@@ -500,14 +500,16 @@
         high, low = split_rounded(edge)
         left = jnp.where(lanes_of(members * rows) < 64, high, low).astype(BF16)
         left = jnp.concatenate([left, left], axis=1)
-        for k in range(levels):
-            out_ref[k] = part_ref[k]
         high, low = w_ref[0:64], w_ref[64:128]
         right = jnp.concatenate([high, high, low, low], axis=0)
-        for m in range(members):
-            added = dot(left[rows * m : rows * m + rows], right)
-            for k in range(levels):
-                out_ref[k] += pert_ref[m, k].astype(F32) * added[:, width * k : width * k + width]
+        for first in range(0, levels, 2):
+            added = dot(left, right[:, width * first : width * (first + 2)])
+            for k in range(first, first + 2):
+                total = part_ref[k]
+                for m in range(members):
+                    block = added[rows * m : rows * m + rows, width * (k - first) : width * (k - first + 1)]
+                    total = total + pert_ref[m, k].astype(F32) * block
+                out_ref[k] = total
 
     return pl.pallas_call(
         kernel,

time: 62.5 us -> 62.1 us (level)
  no operation moved by 1% of the time
where the time goes in v4:
time: 62.1 us; the launch traced here: 61.6 us
  starting transfers between devices  23.7 us (38%)
  Pallas kernels  20 us (32%)
  waiting for transfers between devices  17.1 us (28%)
  other arithmetic  0.74 us (1%)
    all_to_all x1, waiting for transfers between devices, local(): crossed = lax.all_to_all(crossing, 'east', 0, 0)  8.82 us
    all_to_all x1, starting transfers between devices, local(): crossed = lax.all_to_all(crossing, 'east', 0, 0)  8.2 us
    all_to_all x1, starting transfers between devices, local(): gathered = lax.all_to_all(functionals, 'north', 0, 0)  7.6 us
    pallas_call x1, Pallas kernels, own_increment(): pl.pallas_call(kernel, in_specs=[SMEM, HBM] + [VMEM] * 5, out_specs=[VMEM...  5.38 us
    pallas_call x1, Pallas kernels, east_matrices(): pl.pallas_call(kernel, in_specs=[SMEM, SMEM, VMEM], out_specs=[VMEM, VMEM...  4.98 us
    ppermute x1, starting transfers between devices, local(): return increment + lax.ppermute(increment, 'group', [(0, 1), (1, 0)])  4.33 us
    pallas_call x1, Pallas kernels, own_crossing(): pl.pallas_call(kernel, in_specs=[HBM, VMEM, VMEM], out_specs=[VMEM] * 3,...  3.88 us
    all_to_all x1, waiting for transfers between devices, local(): lax.all_to_all(chained, 'north', 0, 0).reshape(levels, 8 * members, width)  3.67 us
  transfers between devices with their start and end apart: 4, of which 4 were waited for; matrix products, arithmetic and copies ran while one was open for 0% of the time, Pallas kernels for 23%

profile of v4, /device:TPU:1, one launch (start us, length us, event | category | flops | bytes accessed | tf_op | source)
XLA Modules:
  0.0 61.6 jit_solution(9117250603947640197)
XLA Ops:
  0.0 0.0 copy-start.2
  0.0 0.0 copy-start.1
  0.0 2.9 %north_functionals.1 = (f32[16,40,128]{2,1,0:T(8,128)}, f32[64,8,128]{2,1,0:T(8,128)}) custom-call(f32[5,8,64]{2,1,0:T(8,128)} %nf_hbm.1, f32[8,8,64,128]{3,2,1,0:T(8,128)} %alpha_hbm.5), custom_call_target="tpu_custom_call" | custom-call | tf_op jit(solution)/shard_map/north_functionals/pallas_call | solution.py:115
  2.9 7.6 %all-to-all-start = ((f32[16,40,128]{2,1,0:T(8,128)}), f32[16,40,128]{2,1,0:T(8,128)S(1)}, u32[]{:S(2)}, u32[]{:S(2)}) async-start(f32[16,40,128]{2,1,0:T(8,128)} %get-tuple-element.21), calls=%async_computation | async-start | bytes 655360 | tf_op jit(solution)/shard_map/all_to_all | solution.py:529
  10.6 0.0 copy-done.2
  10.6 0.0 copy-done.1
  10.6 0.0 copy-start
  10.6 5.0 %east_matrices.1 = (bf16[8,256,128]{2,1,0:T(8,128)(2,1)S(1)}, bf16[8,64,128]{2,1,0:T(8,128)(2,1)S(1)}, bf16[128,1024]{1,0:T(8,128)(2,1)S(1)}) custom-call(s32[1]{0:T(128)} %bitcast.e_ref, f32[5]{0:T(128)S(1)} %copy-done.2, f32[5,8,1024]{2,1,0:T(8,128)S(1)} %copy-done.1), custom_call_target="tpu_custom_call" | custom-call | flops 2000000000 | bytes 4194304 | tf_op jit(solution)/shard_map/east_matrices/pallas_call | solution.py:362
  15.6 3.5 %all-to-all-done.r_ref = f32[16,40,128]{2,1,0:T(8,128)S(1)} async-done(((f32[16,40,128]{2,1,0:T(8,128)}), f32[16,40,128]{2,1,0:T(8,128)S(1)}, u32[]{:S(2)}, u32[]{:S(2)}) %all-to-all-start) | async-done | bytes 327712 | tf_op jit(solution)/shard_map/all_to_all | solution.py:529
  19.0 1.0 %chain_slabs.1 = f32[16,32,128]{2,1,0:T(8,128)} custom-call(f32[16,40,128]{2,1,0:T(8,128)S(1)} %all-to-all-done.r_ref), custom_call_target="tpu_custom_call" | custom-call | tf_op jit(solution)/shard_map/chain_slabs/pallas_call | solution.py:168
  20.0 3.5 %all-to-all-start.1 = ((f32[16,32,128]{2,1,0:T(8,128)}), f32[16,32,128]{2,1,0:T(8,128)S(1)}, u32[]{:S(2)}, u32[]{:S(2)}) async-start(f32[16,32,128]{2,1,0:T(8,128)} %chain_slabs.1), calls=%async_computation.1 | async-start | bytes 524288 | tf_op jit(solution)/shard_map/all_to_all | solution.py:533
  23.6 0.0 copy-done
  23.6 3.9 %own_crossing.1 = (f32[8,32,512]{2,1,0:T(8,128)S(1)}, bf16[8,64,32]{2,1,0:T(8,128)(2,1)S(1)}, bf16[8,32,128]{2,1,0:T(8,128)(2,1)S(1)}) custom-call(f32[8,8,64,128]{3,2,1,0:T(8,128)} %alpha_hbm.5, f32[64,8,128]{2,1,0:T(8,128)S(1)} %copy-done, bf16[8,64,128]{2,1,0:T(8,128)(2,1)S(1)} %get-tuple-element.26.v_ref), custom_call_target="tpu_custom_call" | custom-call | flops 2000000000 | bytes 4194304 | tf_op jit(solution)/shard_map/own_crossing/pallas_call | solution.py:231
  27.5 3.7 %all-to-all-done.1 = f32[16,32,128]{2,1,0:T(8,128)S(1)} async-done(((f32[16,32,128]{2,1,0:T(8,128)}), f32[16,32,128]{2,1,0:T(8,128)S(1)}, u32[]{:S(2)}, u32[]{:S(2)}) %all-to-all-start.1) | async-done | bytes 262176 | tf_op jit(solution)/shard_map/all_to_all | solution.py:533
  31.2 1.3 %north_finish.1 = f32[8,32,512]{2,1,0:T(8,128)} custom-call(f32[8,32,512]{2,1,0:T(8,128)S(1)} %get-tuple-element.27.c0_ref, bf16[8,32,128]{2,1,0:T(8,128)(2,1)S(1)} %get-tuple-element.28.b_ref, f32[8,64,128]{2,1,0:T(8,128)S(1)} %bitcast.2, bf16[8,64,128]{2,1,0:T(8,128)(2,1)S(1)} %get-tuple-element.26.v_ref), custom_call_target="tpu_custom_call" | custom-call | tf_op jit(solution)/shard_map/north_finish/pallas_call | solution.py:427
  32.5 8.2 %all-to-all-start.2 = ((f32[8,32,512]{2,1,0:T(8,128)}), f32[8,32,512]{2,1,0:T(8,128)S(1)}, u32[]{:S(2)}, u32[]{:S(2)}) async-start(f32[8,32,512]{2,1,0:T(8,128)} %north_finish.1), calls=%async_computation.2 | async-start | bytes 1048576 | tf_op jit(solution)/shard_map/all_to_all | solution.py:537
  40.7 5.4 %own_increment.1 = (f32[8,64,128]{2,1,0:T(8,128)S(1)}, bf16[8,8,64,128]{3,2,1,0:T(8,128)(2,1)S(1)}) custom-call(f32[5]{0:T(128)S(1)} %copy-done.2, f32[8,8,64,128]{3,2,1,0:T(8,128)} %alpha_hbm.5, f32[64,8,128]{2,1,0:T(8,128)S(1)} %copy-done, bf16[8,64,32]{2,1,0:T(8,128)(2,1)S(1)} %get-tuple-element.32.u_ref, f32[8,64,128]{2,1,0:T(8,128)S(1)} %bitcast.3, ...), custom_call_target="tpu_custom_call" | custom-call | flops 2000000000 | bytes 4194304 | tf_op jit(solution)/shard_map/own_increment/pallas_call | solution.py:468
  46.1 8.8 %all-to-all-done.2.r_ref = f32[8,32,512]{2,1,0:T(8,128)S(1)} async-done(((f32[8,32,512]{2,1,0:T(8,128)}), f32[8,32,512]{2,1,0:T(8,128)S(1)}, u32[]{:S(2)}, u32[]{:S(2)}) %all-to-all-start.2) | async-done | bytes 524320 | tf_op jit(solution)/shard_map/all_to_all | solution.py:537
  54.9 0.5 finish.1
  55.4 4.3 %collective-permute-start = (f32[8,64,128]{2,1,0:T(8,128)S(1)}, f32[8,64,128]{2,1,0:T(8,128)S(1)}, u32[]{:S(2)}, u32[]{:S(2)}) collective-permute-start(f32[8,64,128]{2,1,0:T(8,128)S(1)} %finish.1), channel_id=1, source_target_pairs={{0,1},{1,0},{2,3},{3,2},{4,5},{5,4},{6,7},{7,6},{8,9},{9,8},{10,11... | collective-permute-start | bytes 786440 | tf_op jit(solution)/shard_map/ppermute | solution.py:540
  59.7 1.2 %collective-permute-done = f32[8,64,128]{2,1,0:T(8,128)S(1)} collective-permute-done((f32[8,64,128]{2,1,0:T(8,128)S(1)}, f32[8,64,128]{2,1,0:T(8,128)S(1)}, u32[]{:S(2)}, u32[]{:S(2)}) %collective-permute-start) | collective-permute-done | bytes 262176 | tf_op jit(solution)/shard_map/ppermute | solution.py:540
  60.9 0.7 %add.3 = f32[8,64,128]{2,1,0:T(8,128)} add(f32[8,64,128]{2,1,0:T(8,128)S(1)} %finish.1, f32[8,64,128]{2,1,0:T(8,128)S(1)} %collective-permute-done) | non-fusion elementwise | flops 65536 | bytes 786432 | tf_op jit(solution)/shard_map/add | solution.py:540
Async XLA Ops:
  0.0 10.6 %copy-start.2 = (f32[5]{0:T(128)S(1)}, f32[5]{0:T(128)}, u32[]{:S(2)}) copy-start(f32[5]{0:T(128)} %taps_ref.3) | copy-start | bytes 64
  0.0 10.6 %copy-start.1 = (f32[5,8,1024]{2,1,0:T(8,128)S(1)}, f32[5,8,1024]{2,1,0:T(8,128)}, u32[]{:S(2)}) copy-start(f32[5,8,1024]{2,1,0:T(8,128)} %ef_ref.1) | copy-start | bytes 491524
  2.9 16.1 %all-to-all-start = ((f32[16,40,128]{2,1,0:T(8,128)}), f32[16,40,128]{2,1,0:T(8,128)S(1)}, u32[]{:S(2)}, u32[]{:S(2)}) async-start(f32[16,40,128]{2,1,0:T(8,128)} %get-tuple-element.21), calls=%async_computation | async-start | bytes 655360 | tf_op jit(solution)/shard_map/all_to_all | solution.py:529
  10.6 13.0 %copy-start = (f32[64,8,128]{2,1,0:T(8,128)S(1)}, f32[64,8,128]{2,1,0:T(8,128)}, u32[]{:S(2)}) copy-start(f32[64,8,128]{2,1,0:T(8,128)} %get-tuple-element.25.s_ref.slab_ref) | copy-start | bytes 786436
  20.0 11.1 %all-to-all-start.1 = ((f32[16,32,128]{2,1,0:T(8,128)}), f32[16,32,128]{2,1,0:T(8,128)S(1)}, u32[]{:S(2)}, u32[]{:S(2)}) async-start(f32[16,32,128]{2,1,0:T(8,128)} %chain_slabs.1), calls=%async_computation.1 | async-start | bytes 524288 | tf_op jit(solution)/shard_map/all_to_all | solution.py:533
  32.5 22.4 %all-to-all-start.2 = ((f32[8,32,512]{2,1,0:T(8,128)}), f32[8,32,512]{2,1,0:T(8,128)S(1)}, u32[]{:S(2)}, u32[]{:S(2)}) async-start(f32[8,32,512]{2,1,0:T(8,128)} %north_finish.1), calls=%async_computation.2 | async-start | bytes 1048576 | tf_op jit(solution)/shard_map/all_to_all | solution.py:537
  55.4 5.5 %collective-permute-start = (f32[8,64,128]{2,1,0:T(8,128)S(1)}, f32[8,64,128]{2,1,0:T(8,128)S(1)}, u32[]{:S(2)}, u32[]{:S(2)}) collective-permute-start(f32[8,64,128]{2,1,0:T(8,128)S(1)} %finish.1), channel_id=1, source_target_pairs={{0,1},{1,0},{2,3},{3,2},{4,5},{5,4},{6,7},{7,6},{8,9},{9,8},{10,11... | collective-permute-start | bytes 786440 | tf_op jit(solution)/shard_map/ppermute | solution.py:540

commit v5 on v4

--- a/solution.py
+++ b/solution.py
@@ -142,7 +142,15 @@
 def chain_slabs(received):
     slabs = received.shape[0]
 
-    def kernel(r_ref, z_ref, v_ref):
+    group = slabs // 4
+
+    def kernel(r_ref, z_hbm, z_ref, v_ref, sems):
+        stores = [
+            pltpu.make_async_copy(
+                z_ref.at[pl.ds(group * j, group)], z_hbm.at[pl.ds(group * j, group)], sems.at[j]
+            )
+            for j in range(4)
+        ]
         state = [jnp.zeros((4, 128), F32)] * 4
         for n in range(slabs):
             maps = r_ref[n, 32:40, :]
@@ -164,13 +172,21 @@
                 for j in range(4):
                     value = value + column[j] * jnp.broadcast_to(pending[m][j : j + 1], (4, 128))
                 pending[m] = value
+            if n % group == 0:
+                stores[n // group].start()
+        for store in stores:
+            store.wait()
 
     return pl.pallas_call(
         kernel,
         in_specs=[VMEM],
-        out_specs=VMEM,
+        out_specs=HBM,
         out_shape=jax.ShapeDtypeStruct((slabs, 32, 128), F32),
-        scratch_shapes=[pltpu.VMEM((slabs, 16, 128), F32)],
+        scratch_shapes=[
+            pltpu.VMEM((slabs, 32, 128), F32),
+            pltpu.VMEM((slabs, 16, 128), F32),
+            pltpu.SemaphoreType.DMA((4,)),
+        ],
         compiler_params=pltpu.CompilerParams(vmem_limit_bytes=8 * MIB),
         name="chain_slabs",
     )(received)

time: 62.1 us -> 62.1 us (level)
  no operation moved by 1% of the time
where the time goes in v5:
time: 62.1 us; the launch traced here: 61.6 us
  starting transfers between devices  23.7 us (38%)
  Pallas kernels  20 us (32%)
  waiting for transfers between devices  17.1 us (28%)
  other arithmetic  0.74 us (1%)
    all_to_all x1, waiting for transfers between devices, local(): crossed = lax.all_to_all(crossing, 'east', 0, 0)  8.82 us
    all_to_all x1, starting transfers between devices, local(): crossed = lax.all_to_all(crossing, 'east', 0, 0)  8.2 us
    all_to_all x1, starting transfers between devices, local(): gathered = lax.all_to_all(functionals, 'north', 0, 0)  7.6 us
    pallas_call x1, Pallas kernels, own_increment(): pl.pallas_call(kernel, in_specs=[SMEM, HBM] + [VMEM] * 5, out_specs=[VMEM...  5.38 us
    pallas_call x1, Pallas kernels, east_matrices(): pl.pallas_call(kernel, in_specs=[SMEM, SMEM, VMEM], out_specs=[VMEM, VMEM...  4.98 us
    ppermute x1, starting transfers between devices, local(): return increment + lax.ppermute(increment, 'group', [(0, 1), (1, 0)])  4.33 us
    pallas_call x1, Pallas kernels, own_crossing(): pl.pallas_call(kernel, in_specs=[HBM, VMEM, VMEM], out_specs=[VMEM] * 3,...  3.88 us
    all_to_all x1, waiting for transfers between devices, local(): lax.all_to_all(chained, 'north', 0, 0).reshape(levels, 8 * members, width)  3.67 us
  transfers between devices with their start and end apart: 4, of which 4 were waited for; matrix products, arithmetic and copies ran while one was open for 0% of the time, Pallas kernels for 23%

profile of v5, /device:TPU:1, one launch (start us, length us, event | category | flops | bytes accessed | tf_op | source)
XLA Modules:
  0.0 61.6 jit_solution(14095897201759253481)
XLA Ops:
  0.0 0.0 copy-start.2
  0.0 0.0 copy-start.1
  0.0 2.9 %north_functionals.1 = (f32[16,40,128]{2,1,0:T(8,128)}, f32[64,8,128]{2,1,0:T(8,128)}) custom-call(f32[5,8,64]{2,1,0:T(8,128)} %nf_hbm.1, f32[8,8,64,128]{3,2,1,0:T(8,128)} %alpha_hbm.5), custom_call_target="tpu_custom_call" | custom-call | tf_op jit(solution)/shard_map/north_functionals/pallas_call | solution.py:115
  2.9 7.6 %all-to-all-start = ((f32[16,40,128]{2,1,0:T(8,128)}), f32[16,40,128]{2,1,0:T(8,128)S(1)}, u32[]{:S(2)}, u32[]{:S(2)}) async-start(f32[16,40,128]{2,1,0:T(8,128)} %get-tuple-element.21), calls=%async_computation | async-start | bytes 655360 | tf_op jit(solution)/shard_map/all_to_all | solution.py:545
  10.6 0.0 copy-done.2
  10.6 0.0 copy-done.1
  10.6 0.0 copy-start
  10.6 5.0 %east_matrices.1 = (bf16[8,256,128]{2,1,0:T(8,128)(2,1)S(1)}, bf16[8,64,128]{2,1,0:T(8,128)(2,1)S(1)}, bf16[128,1024]{1,0:T(8,128)(2,1)S(1)}) custom-call(s32[1]{0:T(128)} %bitcast.e_ref, f32[5]{0:T(128)S(1)} %copy-done.2, f32[5,8,1024]{2,1,0:T(8,128)S(1)} %copy-done.1), custom_call_target="tpu_custom_call" | custom-call | flops 2000000000 | bytes 4194304 | tf_op jit(solution)/shard_map/east_matrices/pallas_call | solution.py:378
  15.6 3.5 %all-to-all-done.r_ref = f32[16,40,128]{2,1,0:T(8,128)S(1)} async-done(((f32[16,40,128]{2,1,0:T(8,128)}), f32[16,40,128]{2,1,0:T(8,128)S(1)}, u32[]{:S(2)}, u32[]{:S(2)}) %all-to-all-start) | async-done | bytes 327712 | tf_op jit(solution)/shard_map/all_to_all | solution.py:545
  19.0 1.0 %chain_slabs.1 = f32[16,32,128]{2,1,0:T(8,128)} custom-call(f32[16,40,128]{2,1,0:T(8,128)S(1)} %all-to-all-done.r_ref), custom_call_target="tpu_custom_call" | custom-call | tf_op jit(solution)/shard_map/chain_slabs/pallas_call | solution.py:180
  20.0 3.5 %all-to-all-start.1 = ((f32[16,32,128]{2,1,0:T(8,128)}), f32[16,32,128]{2,1,0:T(8,128)S(1)}, u32[]{:S(2)}, u32[]{:S(2)}) async-start(f32[16,32,128]{2,1,0:T(8,128)} %chain_slabs.1), calls=%async_computation.1 | async-start | bytes 524288 | tf_op jit(solution)/shard_map/all_to_all | solution.py:549
  23.6 0.0 copy-done
  23.6 3.9 %own_crossing.1 = (f32[8,32,512]{2,1,0:T(8,128)S(1)}, bf16[8,64,32]{2,1,0:T(8,128)(2,1)S(1)}, bf16[8,32,128]{2,1,0:T(8,128)(2,1)S(1)}) custom-call(f32[8,8,64,128]{3,2,1,0:T(8,128)} %alpha_hbm.5, f32[64,8,128]{2,1,0:T(8,128)S(1)} %copy-done, bf16[8,64,128]{2,1,0:T(8,128)(2,1)S(1)} %get-tuple-element.26.v_ref), custom_call_target="tpu_custom_call" | custom-call | flops 2000000000 | bytes 4194304 | tf_op jit(solution)/shard_map/own_crossing/pallas_call | solution.py:247
  27.5 3.7 %all-to-all-done.1 = f32[16,32,128]{2,1,0:T(8,128)S(1)} async-done(((f32[16,32,128]{2,1,0:T(8,128)}), f32[16,32,128]{2,1,0:T(8,128)S(1)}, u32[]{:S(2)}, u32[]{:S(2)}) %all-to-all-start.1) | async-done | bytes 262176 | tf_op jit(solution)/shard_map/all_to_all | solution.py:549
  31.1 1.3 %north_finish.1 = f32[8,32,512]{2,1,0:T(8,128)} custom-call(f32[8,32,512]{2,1,0:T(8,128)S(1)} %get-tuple-element.27.c0_ref, bf16[8,32,128]{2,1,0:T(8,128)(2,1)S(1)} %get-tuple-element.28.b_ref, f32[8,64,128]{2,1,0:T(8,128)S(1)} %bitcast.2, bf16[8,64,128]{2,1,0:T(8,128)(2,1)S(1)} %get-tuple-element.26.v_ref), custom_call_target="tpu_custom_call" | custom-call | tf_op jit(solution)/shard_map/north_finish/pallas_call | solution.py:443
  32.5 8.2 %all-to-all-start.2 = ((f32[8,32,512]{2,1,0:T(8,128)}), f32[8,32,512]{2,1,0:T(8,128)S(1)}, u32[]{:S(2)}, u32[]{:S(2)}) async-start(f32[8,32,512]{2,1,0:T(8,128)} %north_finish.1), calls=%async_computation.2 | async-start | bytes 1048576 | tf_op jit(solution)/shard_map/all_to_all | solution.py:553
  40.7 5.4 %own_increment.1 = (f32[8,64,128]{2,1,0:T(8,128)S(1)}, bf16[8,8,64,128]{3,2,1,0:T(8,128)(2,1)S(1)}) custom-call(f32[5]{0:T(128)S(1)} %copy-done.2, f32[8,8,64,128]{3,2,1,0:T(8,128)} %alpha_hbm.5, f32[64,8,128]{2,1,0:T(8,128)S(1)} %copy-done, bf16[8,64,32]{2,1,0:T(8,128)(2,1)S(1)} %get-tuple-element.32.u_ref, f32[8,64,128]{2,1,0:T(8,128)S(1)} %bitcast.3, ...), custom_call_target="tpu_custom_call" | custom-call | flops 2000000000 | bytes 4194304 | tf_op jit(solution)/shard_map/own_increment/pallas_call | solution.py:484
  46.0 8.8 %all-to-all-done.2.r_ref = f32[8,32,512]{2,1,0:T(8,128)S(1)} async-done(((f32[8,32,512]{2,1,0:T(8,128)}), f32[8,32,512]{2,1,0:T(8,128)S(1)}, u32[]{:S(2)}, u32[]{:S(2)}) %all-to-all-start.2) | async-done | bytes 524320 | tf_op jit(solution)/shard_map/all_to_all | solution.py:553
  54.9 0.5 finish.1
  55.4 4.3 %collective-permute-start = (f32[8,64,128]{2,1,0:T(8,128)S(1)}, f32[8,64,128]{2,1,0:T(8,128)S(1)}, u32[]{:S(2)}, u32[]{:S(2)}) collective-permute-start(f32[8,64,128]{2,1,0:T(8,128)S(1)} %finish.1), channel_id=1, source_target_pairs={{0,1},{1,0},{2,3},{3,2},{4,5},{5,4},{6,7},{7,6},{8,9},{9,8},{10,11... | collective-permute-start | bytes 786440 | tf_op jit(solution)/shard_map/ppermute | solution.py:556
  59.7 1.2 %collective-permute-done = f32[8,64,128]{2,1,0:T(8,128)S(1)} collective-permute-done((f32[8,64,128]{2,1,0:T(8,128)S(1)}, f32[8,64,128]{2,1,0:T(8,128)S(1)}, u32[]{:S(2)}, u32[]{:S(2)}) %collective-permute-start) | collective-permute-done | bytes 262176 | tf_op jit(solution)/shard_map/ppermute | solution.py:556
  60.9 0.7 %add.3 = f32[8,64,128]{2,1,0:T(8,128)} add(f32[8,64,128]{2,1,0:T(8,128)S(1)} %finish.1, f32[8,64,128]{2,1,0:T(8,128)S(1)} %collective-permute-done) | non-fusion elementwise | flops 65536 | bytes 786432 | tf_op jit(solution)/shard_map/add | solution.py:556
Async XLA Ops:
  0.0 10.6 %copy-start.2 = (f32[5]{0:T(128)S(1)}, f32[5]{0:T(128)}, u32[]{:S(2)}) copy-start(f32[5]{0:T(128)} %taps_ref.3) | copy-start | bytes 64
  0.0 10.6 %copy-start.1 = (f32[5,8,1024]{2,1,0:T(8,128)S(1)}, f32[5,8,1024]{2,1,0:T(8,128)}, u32[]{:S(2)}) copy-start(f32[5,8,1024]{2,1,0:T(8,128)} %ef_ref.1) | copy-start | bytes 491524
  2.9 16.1 %all-to-all-start = ((f32[16,40,128]{2,1,0:T(8,128)}), f32[16,40,128]{2,1,0:T(8,128)S(1)}, u32[]{:S(2)}, u32[]{:S(2)}) async-start(f32[16,40,128]{2,1,0:T(8,128)} %get-tuple-element.21), calls=%async_computation | async-start | bytes 655360 | tf_op jit(solution)/shard_map/all_to_all | solution.py:545
  10.6 13.0 %copy-start = (f32[64,8,128]{2,1,0:T(8,128)S(1)}, f32[64,8,128]{2,1,0:T(8,128)}, u32[]{:S(2)}) copy-start(f32[64,8,128]{2,1,0:T(8,128)} %get-tuple-element.25.s_ref.slab_ref) | copy-start | bytes 786436
  20.0 11.1 %all-to-all-start.1 = ((f32[16,32,128]{2,1,0:T(8,128)}), f32[16,32,128]{2,1,0:T(8,128)S(1)}, u32[]{:S(2)}, u32[]{:S(2)}) async-start(f32[16,32,128]{2,1,0:T(8,128)} %chain_slabs.1), calls=%async_computation.1 | async-start | bytes 524288 | tf_op jit(solution)/shard_map/all_to_all | solution.py:549
  32.5 22.4 %all-to-all-start.2 = ((f32[8,32,512]{2,1,0:T(8,128)}), f32[8,32,512]{2,1,0:T(8,128)S(1)}, u32[]{:S(2)}, u32[]{:S(2)}) async-start(f32[8,32,512]{2,1,0:T(8,128)} %north_finish.1), calls=%async_computation.2 | async-start | bytes 1048576 | tf_op jit(solution)/shard_map/all_to_all | solution.py:553
  55.4 5.5 %collective-permute-start = (f32[8,64,128]{2,1,0:T(8,128)S(1)}, f32[8,64,128]{2,1,0:T(8,128)S(1)}, u32[]{:S(2)}, u32[]{:S(2)}) collective-permute-start(f32[8,64,128]{2,1,0:T(8,128)S(1)} %finish.1), channel_id=1, source_target_pairs={{0,1},{1,0},{2,3},{3,2},{4,5},{5,4},{6,7},{7,6},{8,9},{9,8},{10,11... | collective-permute-start | bytes 786440 | tf_op jit(solution)/shard_map/ppermute | solution.py:556
